TPU v7x, 1024 devices: a whole 4x8x16 slice. The times are simulated.
1024 devices in a mesh: owner: 32 (over x, y), replica: 32 (over z, core).
Axes of the slice: x: 4, y: 8, z: 16, core: 2. Of those that a mesh axis runs over, the one named last changes fastest.
Arguments:
- cold_vals: bfloat16 [65536, 768], P('owner'), may hold values from -6 to 6
- cold_scales: float32 [65536, 6], P('owner'), may hold values from 0.25 to 4
- hot_vals: bfloat16 [4096, 768], P('replica'), may hold values from -6 to 6
- hot_scales: float32 [4096, 6], P('replica'), may hold values from 0.25 to 4
- cold_req: int32 [32, 32, 1024], P('owner', 'replica'), may hold values from 0 to 2047
- hot_holder: int32 [32, 32, 256, 1], P('owner', 'replica'), may hold values from 0 to 31; in each aligned block of 256 rows (0 to 255, 256 to 511, ..., all dimensions but the last counted through in order) at most 16 rows name the same one
- hot_slot: int32 [32, 32, 256], P('owner', 'replica'), may hold values from 0 to 127
- self_pos: int32 [32, 32, 256], P('owner', 'replica'), may hold values from 0 to 1279
- nbr_pos: int32 [32, 32, 256, 15], P('owner', 'replica'), may hold values from 0 to 1279
- nbr_count: int32 [32, 32, 256], P('owner', 'replica'), may hold values from 0 to 15
- w_self: bfloat16 [768, 1024], replicated, may hold values from -0.21875 to 0.21875
- w_nbr: bfloat16 [768, 1024], replicated, may hold values from -0.21875 to 0.21875
- bias: float32 [1024], replicated, may hold values from -3 to 3
Outputs:
- hidden: bfloat16 [32, 32, 256, 1024], P('owner', 'replica')
Inputs may be any that keep to these rules, and one draw needn't show every extreme that they name: `cold_req`: each device asks every owner for exactly 32 rows. `hot_holder`: at most 16 of one device's requests name one holder.
All inputs are finite; a program needn't handle non-finite values.
Results may differ from a plain program's by a relative error of at most 0.005.
Values may be sent and summed in bfloat16 or wider, within the bound.
No kernel may reach another device: no remote copies, remote signals or barrier semaphores. Data moves between devices by JAX's collectives and lax.ppermute only.
A program may use at most 64 MiB of HBM per device.

v0:
```python
import jax
import jax.numpy as jnp
from jax import lax
from jax.sharding import PartitionSpec as P

D = 768
F = 15
SB = 128
NB = 6


def dequantize(values, scales):
    count = values.shape[0]
    blocks = values.astype(jnp.float32).reshape(count, NB, SB) * scales[:, :, None]
    return blocks.reshape(count, D).astype(jnp.bfloat16)


def per_device(
    cold_vals,
    cold_scales,
    hot_vals,
    hot_scales,
    cold_req,
    hot_holder,
    hot_slot,
    self_pos,
    nbr_pos,
    nbr_count,
    w_self,
    w_nbr,
    bias,
):
    n_owner = lax.axis_size("owner")
    per_owner = cold_req.shape[2] // n_owner
    asks = cold_req.reshape(n_owner, per_owner)
    serve_wanted = lax.all_to_all(asks, "owner", split_axis=0, concat_axis=0, tiled=True)
    flat = serve_wanted.reshape(-1)
    rows = dequantize(cold_vals[flat], cold_scales[flat]).reshape(serve_wanted.shape + (D,))
    cold_rows = lax.all_to_all(rows, "owner", split_axis=0, concat_axis=0, tiled=True)
    cold_rows = cold_rows.reshape(n_owner * per_owner, D)
    holder = hot_holder.reshape(-1)
    slot = hot_slot.reshape(-1)
    cached = hot_vals.shape[0]
    wanted = holder * cached + slot
    own_rows = dequantize(hot_vals, hot_scales)
    piece = lax.all_gather(own_rows, "replica", axis=0, tiled=True)
    picker = (wanted[:, None] == jnp.arange(piece.shape[0], dtype=jnp.int32)[None, :]).astype(
        jnp.bfloat16
    )
    hot_rows = jnp.dot(picker, piece, preferred_element_type=jnp.float32).astype(jnp.bfloat16)
    pool = jnp.concatenate([cold_rows, hot_rows], axis=0)
    targets = self_pos.reshape(-1)
    neighbours = nbr_pos.reshape(targets.shape[0], F)
    counts = nbr_count.reshape(-1)
    positions = jnp.arange(pool.shape[0], dtype=jnp.int32)[None, :]
    adjacency = jnp.zeros((targets.shape[0], pool.shape[0]), jnp.float32)
    for slot_index in range(F):
        alive = (counts > slot_index).astype(jnp.float32)[:, None]
        adjacency = (
            adjacency
            + (neighbours[:, slot_index][:, None] == positions).astype(jnp.float32) * alive
        )
    total = jnp.dot(adjacency.astype(jnp.bfloat16), pool, preferred_element_type=jnp.float32)
    nbr_mean = (total / jnp.maximum(counts, 1).astype(jnp.float32)[:, None]).astype(jnp.bfloat16)
    selfx = pool[targets]
    mixed = jnp.dot(selfx, w_self, preferred_element_type=jnp.float32)
    mixed = mixed + jnp.dot(nbr_mean, w_nbr, preferred_element_type=jnp.float32) + bias[None, :]
    hidden = jnp.maximum(mixed, 0.0).astype(jnp.bfloat16)
    return hidden.reshape(1, 1, targets.shape[0], w_self.shape[1])


def solution(mesh):
    return jax.shard_map(
        per_device,
        mesh=mesh,
        in_specs=(
            P("owner", None),
            P("owner", None),
            P("replica", None),
            P("replica", None),
            P("owner", "replica", None),
            P("owner", "replica", None, None),
            P("owner", "replica", None),
            P("owner", "replica", None),
            P("owner", "replica", None, None),
            P("owner", "replica", None),
            P(),
            P(),
            P(),
        ),
        out_specs=P("owner", "replica", None, None),
        check_vma=False,
    )
```

profile of v0, /device:TPU:1, one launch (start us, length us, event | category | flops | bytes accessed | tf_op | source)
XLA Modules:
  0.0 140.1 jit_solution(15309633812764023623)
XLA Ops:
  6.5 0.0 copy-start
  6.5 0.0 all-gather.2.cloned.1.call-start
  6.5 1.2 copy.19
  7.8 1.4 %fusion.53 = bf16[128,768]{0,1:T(8,128)(2,1)} fusion(bf16[128,768]{0,1:T(8,128)(2,1)S(1)} %copy.19, f32[128,6]{0,1:T(8,128)} %param.16), kind=kLoop, calls=%fused_computation.56 | loop fusion | flops 294912 | bytes 396288 | tf_op jit(solution)/shard_map/convert_element_type | solution.py:15
  9.2 0.0 all-gather.2.cloned.1.call-update
  9.2 0.5 broadcast.198
  9.7 1.2 reduce.6
  10.9 0.7 all_to_all.9
  11.6 10.5 %all-to-all-start = ((s32[32,1,32]{2,1,0:T(1,128)}), s32[32,1,32]{2,1,0:T(1,128)S(1)}, u32[]{:S(2)}, u32[]{:S(2)}) async-start(s32[32,1,32]{2,1,0:T(1,128)} %all_to_all.9), calls=%async_computation | async-start | bytes 32768 | tf_op jit(solution)/shard_map/all_to_all | solution.py:36
  22.1 2.2 %copy.18 = f32[2048,6]{1,0:T(8,128)} copy(f32[2048,6]{0,1:T(8,128)} %param.14) | data formatting | bytes 98304 | tf_op args[1]
  24.3 6.4 %all-to-all-done = s32[32,1,32]{2,1,0:T(1,128)S(1)} async-done(((s32[32,1,32]{2,1,0:T(1,128)}), s32[32,1,32]{2,1,0:T(1,128)S(1)}, u32[]{:S(2)}, u32[]{:S(2)}) %all-to-all-start) | async-done | bytes 4128 | tf_op jit(solution)/shard_map/all_to_all | solution.py:36
  30.7 0.6 reduce.7
  31.3 0.1 reshape.267
  31.4 5.3 %gather_fusion.1 = f32[1024,6]{1,0:T(8,128)} fusion(f32[2048,6]{1,0:T(8,128)} %copy.18, s32[1024]{0:T(1024)S(1)} %broadcast_clamp_fusion), kind=kCustom, calls=%fused_computation.1 | custom fusion | bytes 53248 | tf_op jit(solution)/shard_map/gather | solution.py:38
  36.6 3.6 %mul.156 = f32[1024,6,128]{2,1,0:T(8,128)} broadcast(f32[1024,6]{1,0:T(8,128)} %gather_fusion.1), dimensions={0,1} | broadcast | bytes 3170304 | tf_op jit(solution)/shard_map/mul | solution.py:14
  40.2 4.8 %mul.157 = f32[32,32,768]{2,1,0:T(8,128)} reshape(f32[1024,6,128]{2,1,0:T(8,128)} %mul.156) | data formatting | bytes 6291456 | tf_op jit(solution)/shard_map/mul | solution.py:14
  45.1 0.0 copy-done
  45.1 5.2 %gather_fusion = bf16[1024,768]{1,0:T(8,128)(2,1)} fusion(bf16[2048,768]{1,0:T(8,128)(2,1)S(1)} %copy-done, s32[1024]{0:T(1024)S(1)} %broadcast_clamp_fusion), kind=kCustom, calls=%fused_computation | custom fusion | bytes 3149824 | tf_op jit(solution)/shard_map/gather | solution.py:38
  50.3 4.2 %fusion.1 = bf16[32,32,768]{2,1,0:T(8,128)(2,1)} fusion(f32[32,32,768]{2,1,0:T(8,128)} %mul.157, bf16[32,32,768]{2,1,0:T(8,128)(2,1)} %bitcast.53), kind=kLoop, calls=%fused_computation.6 | loop fusion | flops 2359296 | bytes 6291456 | tf_op jit(solution)/shard_map/convert_element_type | solution.py:15
  54.5 0.0 copy-start.2
  54.5 0.0 copy-start.6
  54.5 0.0 copy-start.4
  54.5 0.0 copy-start.7
  54.5 0.0 copy-start.3
  54.5 4.8 %all-to-all-start.1 = ((bf16[32,32,768]{2,1,0:T(8,128)(2,1)}), bf16[32,32,768]{2,1,0:T(8,128)(2,1)}, u32[]{:S(2)}, u32[]{:S(2)}) async-start(bf16[32,32,768]{2,1,0:T(8,128)(2,1)} %fusion.1), calls=%async_computation.1 | async-start | bytes 3145728 | tf_op jit(solution)/shard_map/all_to_all | solution.py:39
  59.4 0.0 copy-done.2
  59.4 0.0 copy-done.6
  59.4 0.0 copy-done.4
  59.5 0.6 add.85
  60.0 0.0 copy-done.7
  60.0 0.0 copy-done.3
  60.0 0.6 maximum_convert_fusion
  60.6 0.6 compare_convert_fusion.14
  61.3 0.6 fusion.57
  61.9 49.7 %all-gather.2.cloned.1.call-done = bf16[4096,768]{0,1:T(8,128)(2,1)} async-done(((bf16[128,768]{0,1:T(8,128)(2,1)}), bf16[4096,768]{0,1:T(8,128)(2,1)}) %all-gather.2.cloned.1.call-update) | async-done | bytes 6291472 | tf_op jit(solution)/shard_map/all_gather | solution.py:46
  111.6 4.8 %fusion.7 = bf16[256,768]{1,0:T(8,128)(2,1)S(1)} fusion(bf16[4096,768]{0,1:T(8,128)(2,1)} %all-gather.2.cloned.1.call-done, s32[256]{0:T(256)} %add.85), kind=kOutput, calls=%fused_computation.31 | convolution fusion | flops 1611857920 | bytes 6685696 | tf_op jit(solution)/shard_map/dot_general | solution.py:50
  116.4 0.0 copy-start.1
  116.5 0.0 all-to-all-done.1
  116.5 0.7 copy-done.1
  117.2 2.8 %pad_maximum_fusion = bf16[1280,768]{1,0:T(8,128)(2,1)} fusion(bf16[256,768]{1,0:T(8,128)(2,1)S(1)} %fusion.7, bf16[1024,768]{1,0:T(8,128)(2,1)} %bitcast.2), kind=kLoop, calls=%fused_computation.8 | loop fusion | flops 3932160 | bytes 3932160 | tf_op jit(solution)/shard_map/concatenate | solution.py:51
  120.0 3.2 %gather_fusion.2 = bf16[256,768]{1,0:T(8,128)(2,1)S(1)} fusion(bf16[1280,768]{1,0:T(8,128)(2,1)} %pad_maximum_fusion, s32[1024]{0:T(1024)S(1)} %pad_clamp_fusion), kind=kCustom, calls=%fused_computation.2 | custom fusion | bytes 787456 | tf_op jit(solution)/shard_map/gather | solution.py:65
  123.2 0.0 copy-start.5
  123.2 3.0 %fusion.58 = f32[256,1024]{1,0:T(8,128)} fusion(bf16[256,768]{1,0:T(8,128)(2,1)S(1)} %gather_fusion.2, bf16[768,1024]{1,0:T(8,128)(2,1)} %param.23), kind=kOutput, calls=%fused_computation.82 | convolution fusion | flops 402653184 | bytes 3014656 | tf_op jit(solution)/shard_map/dot_general | solution.py:66
  126.2 0.0 copy-done.5
  126.2 7.0 %fusion.8 = bf16[1,1,256,1024]{3,2,1,0:T(8,128)(2,1)} fusion(f32[256,1024]{1,0:T(8,128)} %fusion.58, bf16[768,1024]{1,0:T(8,128)(2,1)} %param.24, f32[256]{0:T(256)} %bitcast.73, s32[256]{0:T(256)} %bitcast.75, f32[256]{0:T(256)S(1)} %bitcast.60, s32[256]{0:T(256)} %bitcast.76, f32[256]{0:T(256)S(1)} %bitcast.61, s32[256]{0:T(256)} %bitcast.77, ...), kind=kOutput, calls=%fused_computation.32 | convolution fusion | flops 926089216 | bytes 5147648 | tf_op jit(solution)/shard_map/dot_general | solution.py:67
  (6 shorter events, 0.0 us)
Async XLA Ops:
  6.5 38.6 %copy-start = (bf16[2048,768]{1,0:T(8,128)(2,1)S(1)}, bf16[2048,768]{1,0:T(8,128)(2,1)}, u32[]{:S(2)}) copy-start(bf16[2048,768]{1,0:T(8,128)(2,1)} %param.13) | copy-start | bytes 9437188
  6.5 105.1 %all-gather.2.cloned.1.call-start = ((), (), s32[]{:S(2)}) async-start(), calls=%async_computation.2 | async-start | bytes 6488064 | tf_op jit(solution)/shard_map/all_gather | solution.py:46
  11.6 19.1 %all-to-all-start = ((s32[32,1,32]{2,1,0:T(1,128)}), s32[32,1,32]{2,1,0:T(1,128)S(1)}, u32[]{:S(2)}, u32[]{:S(2)}) async-start(s32[32,1,32]{2,1,0:T(1,128)} %all_to_all.9), calls=%async_computation | async-start | bytes 32768 | tf_op jit(solution)/shard_map/all_to_all | solution.py:36
  54.5 4.9 %copy-start.2 = (s32[1,1,256,15]{2,1,3,0:T(1,128)S(1)}, s32[1,1,256,15]{2,1,3,0:T(1,128)}, u32[]{:S(2)}) copy-start(s32[1,1,256,15]{2,1,3,0:T(1,128)} %param.21) | copy-start | bytes 46084
  54.5 4.9 %copy-start.6 = (s32[1,1,256,1]{2,3,1,0:T(1,128)S(1)}, s32[1,1,256,1]{2,3,1,0:T(1,128)}, u32[]{:S(2)}) copy-start(s32[1,1,256,1]{2,3,1,0:T(1,128)} %param.18) | copy-start | bytes 3076
  54.5 4.9 %copy-start.4 = (s32[1,1,256]{2,1,0:T(1,128)S(1)}, s32[1,1,256]{2,1,0:T(1,128)}, u32[]{:S(2)}) copy-start(s32[1,1,256]{2,1,0:T(1,128)} %param.19) | copy-start | bytes 3076
  54.5 5.5 %copy-start.7 = (s32[1,1,256]{2,1,0:T(1,128)S(1)}, s32[1,1,256]{2,1,0:T(1,128)}, u32[]{:S(2)}) copy-start(s32[1,1,256]{2,1,0:T(1,128)} %param.20) | copy-start | bytes 3076
  54.5 5.5 %copy-start.3 = (s32[1,1,256]{2,1,0:T(1,128)S(1)}, s32[1,1,256]{2,1,0:T(1,128)}, u32[]{:S(2)}) copy-start(s32[1,1,256]{2,1,0:T(1,128)} %param.22) | copy-start | bytes 3076
  54.5 61.9 %all-to-all-start.1 = ((bf16[32,32,768]{2,1,0:T(8,128)(2,1)}), bf16[32,32,768]{2,1,0:T(8,128)(2,1)}, u32[]{:S(2)}, u32[]{:S(2)}) async-start(bf16[32,32,768]{2,1,0:T(8,128)(2,1)} %fusion.1), calls=%async_computation.1 | async-start | bytes 3145728 | tf_op jit(solution)/shard_map/all_to_all | solution.py:39
  116.4 0.7 copy-start.1
  123.2 3.0 %copy-start.5 = (f32[1,1,256]{2,1,0:T(1,128)S(1)}, f32[1,1,256]{2,1,0:T(1,128)}, u32[]{:S(2)}) copy-start(f32[1,1,256]{2,1,0:T(1,128)} %get-tuple-element.23) | copy-start | bytes 3076
Sparse Core Ops, SparseCore 0:
  10.0 101.6 all-gather.1
where the time goes:
time: 141 us; the launch traced here: 140 us
  waiting for transfers between devices  56.1 us (40%)
  local copies, waits for them, and re-layouts  28.2 us (20%)
  starting transfers between devices  15.3 us (11%)
  matrix products  14.8 us (10%)
  between operations  13.6 us (10%)
  other arithmetic  12.1 us (9%)
    all_gather x1, waiting for transfers between devices, per_device(): piece = lax.all_gather(own_rows, 'replica', axis=0, tiled=True)  49.7 us
    all_to_all x1, starting transfers between devices, per_device(): lax.all_to_all(asks, 'owner', split_axis=0, concat_axis=0, tiled=True)  10.5 us
    mul x2, local copies, waits for them, and re-layouts, dequantize(): values.astype(jnp.float32).reshape(count, NB, SB) * scales[:, :, None]  8.43 us
    dot_general x1, matrix products, per_device(): jnp.dot(nbr_mean, w_nbr, preferred_element_type=jnp.float32)  7.04 us
    all_to_all x1, waiting for transfers between devices, per_device(): lax.all_to_all(asks, 'owner', split_axis=0, concat_axis=0, tiled=True)  6.35 us
    convert_element_type x2, other arithmetic, dequantize(): return blocks.reshape(count, D).astype(jnp.bfloat16)  5.62 us
    gather x1, local copies, waits for them, and re-layouts, per_device(): cold_scales[flat]  5.25 us
    gather x1, local copies, waits for them, and re-layouts, per_device(): cold_vals[flat]  5.22 us
  transfers between devices with their start and end apart: 3, of which 2 were waited for; matrix products, arithmetic and copies ran while one was open for 25% of the time, Pallas kernels for 0%

commit v1 on v0

v1 whole, which is shorter than its diff:
```python
import jax
import jax.numpy as jnp
from jax import lax
from jax.experimental import pallas as pl
from jax.experimental.pallas import tpu as pltpu
from jax.sharding import PartitionSpec as P

D = 768
F = 15
SB = 128
NB = 6
HCAP = 16
LANES = 128
MIB = 1024 * 1024
F32 = jnp.float32
BF16 = jnp.bfloat16
I32 = jnp.int32


def iota(shape, axis):
    return lax.broadcasted_iota(I32, shape, axis)


def call(body, outs, ins, scalars=0, scratch=(), vmem=16, flops=0, moved=0):
    smem = pl.BlockSpec(memory_space=pltpu.SMEM)
    full = pl.BlockSpec(memory_space=pltpu.VMEM)
    many = isinstance(outs, (list, tuple))
    return pl.pallas_call(
        body,
        out_shape=outs,
        in_specs=[smem] * scalars + [full] * (len(ins) - scalars),
        out_specs=[full] * len(outs) if many else full,
        scratch_shapes=list(scratch),
        compiler_params=pltpu.CompilerParams(vmem_limit_bytes=vmem * MIB),
        cost_estimate=pl.CostEstimate(flops=flops, bytes_accessed=moved, transcendentals=0),
    )(*ins)


def dequantize_kernel(vals_ref, scales_ref, out_ref):
    def chunk(at, carry):
        rows = pl.ds(pl.multiple_of(at * LANES, LANES), LANES)
        across = scales_ref[:, rows]
        square = jnp.concatenate([across, jnp.zeros((LANES - NB, LANES), F32)], axis=0)
        down = square.T
        for block in range(NB):
            cols = slice(block * SB, (block + 1) * SB)
            out_ref[rows, cols] = (
                vals_ref[rows, cols].astype(F32) * down[:, block : block + 1]
            ).astype(BF16)
        return carry

    lax.fori_loop(0, vals_ref.shape[0] // LANES, chunk, 0)


def dequantize(vals, scales):
    rows = vals.shape[0]
    return call(
        dequantize_kernel,
        jax.ShapeDtypeStruct((rows, D), BF16),
        [vals, scales.T],
        vmem=12,
        flops=rows * D,
        moved=rows * D * 4,
    )


def server_of(holder):
    return (holder // 2) % 8


def local_of(holder, core):
    return (holder // 16) * 2 + jnp.bitwise_xor(holder % 2, core)


def ask_kernel(core_ref, cold_ref, holder_ref, slot_ref, ask_ref, place_ref):
    core = core_ref[0]
    n = holder_ref.shape[1]
    across = jnp.broadcast_to(holder_ref[...], (n, n))
    down = across.T
    earlier = (across == down) & (iota((n, n), 1) < iota((n, n), 0))
    rank = jnp.sum(earlier.astype(F32), axis=1, keepdims=True).astype(I32)
    down = down[:, :LANES]
    lane = local_of(down, core) * HCAP + rank
    place_ref[...] = server_of(down) * 64 + lane
    owners = ask_ref.shape[0]
    server = iota((owners, n), 0)
    server = (server // 8) * 2 + server % 2
    named = server_of(jnp.broadcast_to(holder_ref[...], (owners, n))) == server
    slots = jnp.broadcast_to(slot_ref[...], (owners, n)).astype(F32)
    left = jnp.where(named, slots, 0.0).astype(BF16)
    right = (lane + 32 == iota((n, LANES), 1)).astype(F32).astype(BF16)
    hot = jnp.dot(left, right, preferred_element_type=F32).astype(I32)
    column = iota((1, LANES), 1)
    base = jnp.clip((column - 32) // HCAP, 0, 3) * LANES
    for p in range(owners):
        cold = cold_ref[:, (p // 4) * LANES : (p // 4 + 1) * LANES]
        if p % 4:
            cold = pltpu.roll(cold, LANES - 32 * (p % 4), 1)
        ask_ref[p] = jnp.where(column < 32, cold, hot[p : p + 1] + base)


def transposed(rows):
    n = rows.shape[0]
    if n < LANES:
        rows = jnp.concatenate([rows, jnp.zeros((LANES - n, LANES), I32)], axis=0)
    return rows.T


def serve_cold_kernel(asked_ref, table_ref, out_ref):
    asks = transposed(jnp.concatenate([asked_ref[p] for p in range(32)], axis=0))
    rows = table_ref.shape[0]
    group = 8
    for first in range(0, 32, group):
        mask = jnp.concatenate(
            [
                (asks[:32, p : p + 1] == iota((32, rows), 1)).astype(F32).astype(BF16)
                for p in range(first, first + group)
            ],
            axis=0,
        )
        out_ref[first * 32 : (first + group) * 32, :] = jnp.dot(
            mask, table_ref[...], preferred_element_type=F32
        ).astype(BF16)


def serve_hot_kernel(pair_ref, asked_ref, u_ref, u2_ref, d_ref, d2_ref, out_ref):
    pair = pair_ref[0]
    asks = transposed(
        jnp.concatenate([asked_ref[x * 8 + 2 * pair + b] for x in range(4) for b in range(2)], axis=0)
    )
    for q in range(8):
        for piece, ref in enumerate((u_ref, u2_ref, d_ref, d2_ref)):
            at = 32 + piece * HCAP
            mask = asks[at : at + HCAP, q : q + 1] == iota((HCAP, LANES), 1) + piece * LANES
            out_ref[q * 64 + piece * HCAP : q * 64 + (piece + 1) * HCAP, :] = jnp.dot(
                mask.astype(F32).astype(BF16), ref[...], preferred_element_type=F32
            ).astype(BF16)


def weigh_kernel(self_ref, nbr_ref, count_ref, place_ref, cold_ref, hot_ref, divisor_ref):
    n = self_ref.shape[1]
    count = count_ref[...]
    own = self_ref[...]
    live = [jnp.where(count > f, nbr_ref[f], -1) for f in range(F)]

    def chunk(at):
        position = iota((LANES, n), 0) + at * LANES
        picked = (own == position).astype(F32)
        times = jnp.zeros((LANES, n), F32)
        for f in range(F):
            times = times + (live[f] == position).astype(F32)
        return picked.T.astype(BF16), times.T.astype(BF16)

    n_cold = cold_ref.shape[1] // LANES
    for at in range(n_cold):
        picked, times = chunk(at)
        cols = slice(at * LANES, (at + 1) * LANES)
        cold_ref[:n, cols] = picked
        cold_ref[n:, cols] = times
    slots = hot_ref.shape[1]
    pieces = []
    for at in range(place_ref.shape[0] // LANES):
        picked, times = chunk(n_cold + at)
        place = place_ref[at * LANES : (at + 1) * LANES, :]
        place = jnp.concatenate([place] * (slots // LANES), axis=1)
        spread = (place == iota((LANES, slots), 1)).astype(F32).astype(BF16)
        both = jnp.concatenate([picked, times], axis=0)
        pieces.append(jnp.dot(both, spread, preferred_element_type=F32))
    hot_ref[...] = sum(pieces[1:], pieces[0]).astype(BF16)
    divisor = jnp.maximum(count, 1).astype(F32)
    divisor_ref[...] = jnp.broadcast_to(divisor, (LANES, n)).T


def cold_sum_kernel(weight_ref, rows_ref, out_ref):
    out_ref[...] = jnp.dot(weight_ref[...], rows_ref[...], preferred_element_type=F32)


def layer_kernel(part_ref, weight_ref, rows_ref, divisor_ref, w_self_ref, w_nbr_ref, bias_ref, out_ref):
    n = out_ref.shape[0]
    total = part_ref[...] + jnp.dot(weight_ref[...], rows_ref[...], preferred_element_type=F32)
    own = total[:n].astype(BF16)
    divisor = jnp.concatenate([divisor_ref[...]] * (D // LANES), axis=1)
    mean = (total[n:] / divisor).astype(BF16)
    mixed = jnp.dot(own, w_self_ref[...], preferred_element_type=F32)
    mixed = mixed + jnp.dot(mean, w_nbr_ref[...], preferred_element_type=F32) + bias_ref[...]
    out_ref[...] = jnp.maximum(mixed, 0.0).astype(BF16)


def device_at(owner, z, core):
    return owner * 32 + (z % 16) * 2 + core


def home(owner):
    return (owner // 8) * 2 + owner % 2


def shifted(array, starts, step):
    pairs = [
        (device_at(o, home(o) + s, c), device_at(o, home(o) + s + step, c))
        for o in range(32)
        for s in starts
        for c in range(2)
    ]
    return lax.ppermute(array, ("owner", "replica"), pairs)


def other_core(array):
    return lax.ppermute(array, ("owner", "replica"), [(i, i ^ 1) for i in range(1024)])


def per_device(
    cold_vals,
    cold_scales,
    hot_vals,
    hot_scales,
    cold_req,
    hot_holder,
    hot_slot,
    self_pos,
    nbr_pos,
    nbr_count,
    w_self,
    w_nbr,
    bias,
):
    owner = lax.axis_index("owner")
    replica = lax.axis_index("replica")
    core = replica % 2
    steps = (replica // 2 - home(owner)) % 16

    own = dequantize(hot_vals, hot_scales)
    ask, place = call(
        ask_kernel,
        [jax.ShapeDtypeStruct((32, 1, LANES), I32), jax.ShapeDtypeStruct((256, LANES), I32)],
        [core.reshape(1), cold_req.reshape(1, 1024), hot_holder.reshape(1, 256), hot_slot.reshape(1, 256)],
        scalars=1,
    )
    up = jnp.where(steps == 0, own, 0)
    down = jnp.where(steps == 8, own, 0)
    up = up + shifted(own, (0,), 8)
    down = down + shifted(own, (8,), -8)

    asked = lax.all_to_all(ask, "owner", split_axis=0, concat_axis=0, tiled=True)
    table = dequantize(cold_vals, cold_scales)
    asked, up, down = lax.optimization_barrier((asked, up, down))
    served = call(
        serve_cold_kernel,
        jax.ShapeDtypeStruct((1024, D), BF16),
        [asked, table],
        vmem=24,
        flops=2 * 1024 * 2048 * D,
        moved=5 * MIB,
    )
    cold_rows = lax.all_to_all(served.reshape(32, 32, D), "owner", split_axis=0, concat_axis=0, tiled=True)

    for step, starts in ((4, (0, 8)), (2, (0, 4, 8, 12)), (1, (0, 2, 4, 6, 8, 10, 12, 14))):
        from_below, from_above = shifted(up, starts, step), shifted(down, starts, -step)
        up, down = up + from_below, down + from_above
    up2, down2 = other_core(up), other_core(down)
    hot_served = call(
        serve_hot_kernel,
        jax.ShapeDtypeStruct((512, D), BF16),
        [((owner % 8) // 2).reshape(1), asked, up, up2, down, down2],
        scalars=1,
        flops=2 * 512 * 128 * D,
        moved=2 * MIB,
    )

    weight_cold, weight_hot, divisor = call(
        weigh_kernel,
        [
            jax.ShapeDtypeStruct((512, 1024), BF16),
            jax.ShapeDtypeStruct((512, 512), BF16),
            jax.ShapeDtypeStruct((256, LANES), F32),
        ],
        [
            self_pos.reshape(1, 256),
            jnp.transpose(nbr_pos.reshape(256, F)).reshape(F, 1, 256),
            nbr_count.reshape(1, 256),
            place,
        ],
        flops=16 * 512 * 1280,
        moved=2 * MIB,
    )

    hot_served, cold_rows = lax.optimization_barrier((hot_served, cold_rows))
    groups = [[x * 8 + 2 * pair + b for x in range(4) for b in range(2)] for pair in range(4)]
    hot_rows = lax.all_to_all(
        hot_served.reshape(8, 64, D), "owner", split_axis=0, concat_axis=0, tiled=True, axis_index_groups=groups
    )
    part = call(
        cold_sum_kernel,
        jax.ShapeDtypeStruct((512, D), F32),
        [weight_cold, cold_rows.reshape(1024, D)],
        flops=2 * 512 * 1024 * D,
        moved=4 * MIB,
    )
    hidden = call(
        layer_kernel,
        jax.ShapeDtypeStruct((256, 1024), BF16),
        [part, weight_hot, hot_rows.reshape(512, D), divisor, w_self, w_nbr, bias.reshape(1, 1024)],
        vmem=24,
        flops=2 * 512 * 512 * D + 4 * 256 * D * 1024,
        moved=6 * MIB,
    )
    return hidden.reshape(1, 1, 256, 1024)


def solution(mesh):
    return jax.shard_map(
        per_device,
        mesh=mesh,
        in_specs=(
            P("owner", None),
            P("owner", None),
            P("replica", None),
            P("replica", None),
            P("owner", "replica", None),
            P("owner", "replica", None, None),
            P("owner", "replica", None),
            P("owner", "replica", None),
            P("owner", "replica", None, None),
            P("owner", "replica", None),
            P(),
            P(),
            P(),
        ),
        out_specs=P("owner", "replica", None, None),
        check_vma=False,
    )
```

time: 141 us -> 127 us (0.901)
  the two profiles are of different devices: /device:TPU:1 before, /device:TPU:16 now
where the time goes in v1:
time: 127 us; the launch traced here: 126 us
  starting transfers between devices  74.1 us (58%)
  Pallas kernels  18.9 us (15%)
  waiting for transfers between devices  18.1 us (14%)
  local copies, waits for them, and re-layouts  12.2 us (10%)
  other arithmetic  2.1 us (2%)
    ppermute x8, starting transfers between devices, shifted(): return lax.ppermute(array, ('owner', 'replica'), pairs)  43 us
    pallas_call x8, Pallas kernels, call(): pl.pallas_call(body, out_shape=outs, in_specs=[smem] * scalars + [full] *...  18.9 us
    unnamed x37, local copies, waits for them, and re-layouts  12.2 us
    all_to_all x1, starting transfers between devices, per_device(): lax.all_to_all(served.reshape(32, 32, D), 'owner', split_axis=0, concat_a...  9.92 us
    all_to_all x1, starting transfers between devices, per_device(): lax.all_to_all(hot_served.reshape(8, 64, D), 'owner', split_axis=0, conca...  9.21 us
    all_to_all x1, waiting for transfers between devices, per_device(): lax.all_to_all(hot_served.reshape(8, 64, D), 'owner', split_axis=0, conca...  9.08 us
    ppermute x8, waiting for transfers between devices, shifted(): return lax.ppermute(array, ('owner', 'replica'), pairs)  7.97 us
    all_to_all x1, starting transfers between devices, per_device(): lax.all_to_all(ask, 'owner', split_axis=0, concat_axis=0, tiled=True)  7.59 us
  transfers between devices with their start and end apart: 13, of which 5 were waited for; matrix products, arithmetic and copies ran while one was open for 2% of the time, Pallas kernels for 9%

profile of v1, /device:TPU:16, one launch (start us, length us, event | category | flops | bytes accessed | tf_op | source)
XLA Modules:
  0.0 125.7 jit_solution(5588626287330089528)
XLA Ops:
  0.0 0.9 copy-done.6
  0.9 0.7 copy-done.8
  1.6 0.3 shard_map.129
  1.9 20.0 %collective-permute-start = (bf16[128,768]{1,0:T(8,128)(2,1)S(1)}, bf16[128,768]{1,0:T(8,128)(2,1)}, u32[]{:S(2)}, u32[]{:S(2)}) collective-permute-start(bf16[128,768]{1,0:T(8,128)(2,1)S(1)} %shard_map.129), channel_id=1, source_target_pairs={{0,16},{1,17},{34,50},{35,51},{64,80},{65,81},{98,114},{99,115},{1... | collective-permute-start | bytes 589832 | tf_op jit(solution)/shard_map/ppermute | solution.py:204
  21.9 1.3 %collective-permute-start.1 = (bf16[128,768]{1,0:T(8,128)(2,1)S(1)}, bf16[128,768]{1,0:T(8,128)(2,1)}, u32[]{:S(2)}, u32[]{:S(2)}) collective-permute-start(bf16[128,768]{1,0:T(8,128)(2,1)S(1)} %shard_map.129), channel_id=1, source_target_pairs={{16,0},{17,1},{50,34},{51,35},{80,64},{81,65},{114,98},{115,99},{1... | collective-permute-start | bytes 589832 | tf_op jit(solution)/shard_map/ppermute | solution.py:204
  23.2 0.0 copy-start.9
  23.3 0.7 copy-done.9
  23.9 0.7 copy-done.13
  24.6 0.7 copy-done.14
  25.3 1.1 shard_map.127
  26.4 7.6 %all-to-all-start = ((s32[32,1,128]{2,1,0:T(1,128)}), s32[32,1,128]{2,1,0:T(1,128)S(1)}, u32[]{:S(2)}, u32[]{:S(2)}) async-start(s32[32,1,128]{2,1,0:T(1,128)} %get-tuple-element.17), calls=%async_computation | async-start | bytes 32768 | tf_op jit(solution)/shard_map/all_to_all | solution.py:243
  34.0 0.0 copy-start
  34.0 1.9 %copy-done = bf16[2048,768]{1,0:T(8,128)(2,1)S(1)} copy-done((bf16[2048,768]{1,0:T(8,128)(2,1)S(1)}, bf16[2048,768]{1,0:T(8,128)(2,1)}, u32[]{:S(2)}) %copy-start) | copy-done | bytes 3145752
  35.9 0.8 copy-done.7
  36.8 4.6 %shard_map.131.table_ref = bf16[2048,768]{1,0:T(8,128)(2,1)S(1)} custom-call(bf16[2048,768]{1,0:T(8,128)(2,1)S(1)} %copy-done, f32[6,2048]{1,0:T(8,128)S(1)} %bitcast.22), custom_call_target="tpu_custom_call" | custom-call | flops 1572864 | bytes 6291456 | tf_op jit(solution)/shard_map/pallas_call | solution.py:28
  41.4 0.0 collective-permute-done
  41.4 0.0 collective-permute-done.1
  41.4 1.8 %select_add_fusion = (bf16[128,768]{1,0:T(8,128)(2,1)}, bf16[128,768]{1,0:T(8,128)(2,1)}) fusion(bf16[128,768]{1,0:T(8,128)(2,1)} %collective-permute-done.1, bf16[128,768]{1,0:T(8,128)(2,1)S(1)} %shard_map.129, pred[]{:T(512)S(6)} %eq.12, bf16[128,768]{1,0:T(8,128)(2,1)} %collective-permute-done, pred[]{:T(512)S(6)} %eq.11), kind=kLoop, calls=%fused_computation | loop fusion | flops 393216 | bytes 983042 | tf_op jit(solution)/shard_map/add | solution.py:241
  43.2 0.0 all-to-all-done.asked_ref
  43.2 3.5 %shard_map.132 = bf16[1024,768]{1,0:T(8,128)(2,1)S(1)} custom-call(s32[32,1,128]{2,1,0:T(1,128)S(1)} %all-to-all-done.asked_ref, bf16[2048,768]{1,0:T(8,128)(2,1)S(1)} %shard_map.131.table_ref), custom_call_target="tpu_custom_call" | custom-call | flops 3221225472 | bytes 5242880 | tf_op jit(solution)/shard_map/pallas_call | solution.py:28
  46.8 1.2 copy-done.1
  47.9 9.9 %all-to-all-start.1 = ((bf16[32,32,768]{2,1,0:T(8,128)(2,1)}), bf16[32,32,768]{2,1,0:T(8,128)(2,1)S(1)}, u32[]{:S(2)}, u32[]{:S(2)}) async-start(bf16[32,32,768]{2,1,0:T(8,128)(2,1)} %bitcast.21), calls=%async_computation.1 | async-start | bytes 3145728 | tf_op jit(solution)/shard_map/all_to_all | solution.py:254
  57.9 15.2 %collective-permute-start.6 = (bf16[128,768]{1,0:T(8,128)(2,1)S(1)}, bf16[128,768]{1,0:T(8,128)(2,1)S(1)}, u32[]{:S(2)}, u32[]{:S(2)}) collective-permute-start(bf16[128,768]{1,0:T(8,128)(2,1)S(1)} %copy-done.16), channel_id=1, source_target_pairs={{0,24},{1,25},{16,8},{17,9},{34,58},{35,59},{50,42},{51,43},{64,88... | collective-permute-start | bytes 589832 | tf_op jit(solution)/shard_map/ppermute | solution.py:204
  73.1 1.3 %collective-permute-start.2 = (bf16[128,768]{1,0:T(8,128)(2,1)S(1)}, bf16[128,768]{1,0:T(8,128)(2,1)S(1)}, u32[]{:S(2)}, u32[]{:S(2)}) collective-permute-start(bf16[128,768]{1,0:T(8,128)(2,1)S(1)} %copy-done.15), channel_id=1, source_target_pairs={{0,8},{1,9},{16,24},{17,25},{34,42},{35,43},{50,58},{51,59},{64,72... | collective-permute-start | bytes 589832 | tf_op jit(solution)/shard_map/ppermute | solution.py:204
  74.4 2.8 %collective-permute-done.6 = bf16[128,768]{1,0:T(8,128)(2,1)S(1)} collective-permute-done((bf16[128,768]{1,0:T(8,128)(2,1)S(1)}, bf16[128,768]{1,0:T(8,128)(2,1)S(1)}, u32[]{:S(2)}, u32[]{:S(2)}) %collective-permute-start.6) | collective-permute-done | bytes 196640 | tf_op jit(solution)/shard_map/ppermute | solution.py:204
  77.3 1.3 %collective-permute-start.7 = (bf16[128,768]{1,0:T(8,128)(2,1)S(1)}, bf16[128,768]{1,0:T(8,128)(2,1)S(1)}, u32[]{:S(2)}, u32[]{:S(2)}) collective-permute-start(bf16[128,768]{1,0:T(8,128)(2,1)S(1)} %add.53), channel_id=1, source_target_pairs={{0,28},{1,29},{8,4},{9,5},{16,12},{17,13},{24,20},{25,21},{34,62},... | collective-permute-start | bytes 589832 | tf_op jit(solution)/shard_map/ppermute | solution.py:204
  78.6 1.3 %collective-permute-start.3 = (bf16[128,768]{1,0:T(8,128)(2,1)S(1)}, bf16[128,768]{1,0:T(8,128)(2,1)S(1)}, u32[]{:S(2)}, u32[]{:S(2)}) collective-permute-start(bf16[128,768]{1,0:T(8,128)(2,1)S(1)} %add.50), channel_id=1, source_target_pairs={{0,4},{1,5},{8,12},{9,13},{16,20},{17,21},{24,28},{25,29},{34,38},... | collective-permute-start | bytes 589832 | tf_op jit(solution)/shard_map/ppermute | solution.py:204
  79.9 3.4 %collective-permute-done.7 = bf16[128,768]{1,0:T(8,128)(2,1)S(1)} collective-permute-done((bf16[128,768]{1,0:T(8,128)(2,1)S(1)}, bf16[128,768]{1,0:T(8,128)(2,1)S(1)}, u32[]{:S(2)}, u32[]{:S(2)}) %collective-permute-start.7) | collective-permute-done | bytes 196640 | tf_op jit(solution)/shard_map/ppermute | solution.py:204
  83.4 1.3 %collective-permute-start.8 = (bf16[128,768]{1,0:T(8,128)(2,1)S(1)}, bf16[128,768]{1,0:T(8,128)(2,1)S(1)}, u32[]{:S(2)}, u32[]{:S(2)}) collective-permute-start(bf16[128,768]{1,0:T(8,128)(2,1)S(1)} %add.54), channel_id=1, source_target_pairs={{0,30},{1,31},{4,2},{5,3},{8,6},{9,7},{12,10},{13,11},{16,14},{17,... | collective-permute-start | bytes 589832 | tf_op jit(solution)/shard_map/ppermute | solution.py:204
  84.7 0.0 collective-permute-done.3
  84.7 1.3 %collective-permute-start.4 = (bf16[128,768]{1,0:T(8,128)(2,1)S(1)}, bf16[128,768]{1,0:T(8,128)(2,1)S(1)}, u32[]{:S(2)}, u32[]{:S(2)}) collective-permute-start(bf16[128,768]{1,0:T(8,128)(2,1)S(1)} %add.51), channel_id=1, source_target_pairs={{0,2},{1,3},{4,6},{5,7},{8,10},{9,11},{12,14},{13,15},{16,18},{17,... | collective-permute-start | bytes 589832 | tf_op jit(solution)/shard_map/ppermute | solution.py:204
  86.0 1.8 %collective-permute-done.8 = bf16[128,768]{1,0:T(8,128)(2,1)S(1)} collective-permute-done((bf16[128,768]{1,0:T(8,128)(2,1)S(1)}, bf16[128,768]{1,0:T(8,128)(2,1)S(1)}, u32[]{:S(2)}, u32[]{:S(2)}) %collective-permute-start.8) | collective-permute-done | bytes 196640 | tf_op jit(solution)/shard_map/ppermute | solution.py:204
  87.9 1.9 %collective-permute-start.9 = (bf16[128,768]{1,0:T(8,128)(2,1)S(1)}, bf16[128,768]{1,0:T(8,128)(2,1)S(1)}, u32[]{:S(2)}, u32[]{:S(2)}) collective-permute-start(bf16[128,768]{1,0:T(8,128)(2,1)S(1)} %add.55.d_ref), channel_id=1, source_target_pairs={{0,1},{1,0},{2,3},{3,2},{4,5},{5,4},{6,7},{7,6},{8,9},{9,8},{10,11... | collective-permute-start | bytes 589832 | tf_op jit(solution)/shard_map/ppermute | solution.py:208
  89.8 0.0 collective-permute-done.4
  89.9 2.4 %collective-permute-start.5 = (bf16[128,768]{1,0:T(8,128)(2,1)S(1)}, bf16[128,768]{1,0:T(8,128)(2,1)S(1)}, u32[]{:S(2)}, u32[]{:S(2)}) collective-permute-start(bf16[128,768]{1,0:T(8,128)(2,1)S(1)} %add.52.u_ref), channel_id=1, source_target_pairs={{0,1},{1,0},{2,3},{3,2},{4,5},{5,4},{6,7},{7,6},{8,9},{9,8},{10,11... | collective-permute-start | bytes 589832 | tf_op jit(solution)/shard_map/ppermute | solution.py:208
  92.3 0.0 collective-permute-done.9.d2_ref
  92.3 1.0 collective-permute-done.5.u2_ref
  93.3 2.0 %shard_map.130 = bf16[512,768]{1,0:T(8,128)(2,1)} custom-call(s32[1]{0:T(128)} %bitcast.7.pair_ref, s32[32,1,128]{2,1,0:T(1,128)S(1)} %all-to-all-done.asked_ref, bf16[128,768]{1,0:T(8,128)(2,1)S(1)} %add.52.u_ref, bf16[128,768]{1,0:T(8,128)(2,1)S(1)} %collective-permute-done.5.u2_ref, bf16[128,768]{1,0:T(8,128)(2,1)S(1)} %add.55.d_ref, ...), custom_call_target="tpu_custom_call" | custom-call | flops 100663296 | bytes 2097152 | tf_op jit(solution)/shard_map/pallas_call | solution.py:28
  95.3 9.2 %all-to-all-start.2 = ((bf16[8,64,768]{2,1,0:T(8,128)(2,1)}), bf16[8,64,768]{2,1,0:T(8,128)(2,1)}, u32[]{:S(2)}, u32[]{:S(2)}) async-start(bf16[8,64,768]{2,1,0:T(8,128)(2,1)} %bitcast.12), calls=%async_computation.2 | async-start | bytes 1572864 | tf_op jit(solution)/shard_map/all_to_all | solution.py:288
  104.6 2.4 %shard_map.128 = (bf16[512,1024]{1,0:T(8,128)(2,1)S(1)}, bf16[512,512]{1,0:T(8,128)(2,1)S(1)}, f32[256,128]{1,0:T(8,128)S(1)}) custom-call(s32[1,256]{1,0:T(1,128)S(1)} %bitcast.26, s32[15,1,256]{2,1,0:T(1,128)S(1)} %reshape.47.nbr_ref, s32[1,256]{1,0:T(1,128)S(1)} %bitcast.27, s32[256,128]{1,0:T(8,128)S(1)} %get-tuple-element.15.place_ref), custom_call_target="tpu_custom_call" | custom-call | flops 10485760 | bytes 2097152 | tf_op jit(solution)/shard_map/pallas_call | solution.py:28
  107.0 0.0 copy-start.4
  107.0 0.8 copy-done.4
  107.8 1.0 shard_map.133.part_ref
  108.7 9.1 %all-to-all-done.2 = bf16[8,64,768]{2,1,0:T(8,128)(2,1)} async-done(((bf16[8,64,768]{2,1,0:T(8,128)(2,1)}), bf16[8,64,768]{2,1,0:T(8,128)(2,1)}, u32[]{:S(2)}, u32[]{:S(2)}) %all-to-all-start.2) | async-done | bytes 786464 | tf_op jit(solution)/shard_map/all_to_all | solution.py:288
  117.8 1.4 %copy-done.2 = bf16[768,1024]{1,0:T(8,128)(2,1)S(1)} copy-done((bf16[768,1024]{1,0:T(8,128)(2,1)S(1)}, bf16[768,1024]{1,0:T(8,128)(2,1)}, u32[]{:S(2)}) %copy-start.2) | copy-done | bytes 1572888
  119.2 1.4 %copy-done.3 = bf16[768,1024]{1,0:T(8,128)(2,1)S(1)} copy-done((bf16[768,1024]{1,0:T(8,128)(2,1)S(1)}, bf16[768,1024]{1,0:T(8,128)(2,1)}, u32[]{:S(2)}) %copy-start.3) | copy-done | bytes 1572888
  120.6 1.0 copy-done.5
  121.7 4.0 %shard_map.134 = bf16[256,1024]{1,0:T(8,128)(2,1)} custom-call(f32[512,768]{1,0:T(8,128)S(1)} %shard_map.133.part_ref, bf16[512,512]{1,0:T(8,128)(2,1)S(1)} %copy-done.5, bf16[512,768]{1,0:T(8,128)(2,1)} %bitcast.13.rows_ref, f32[256,128]{1,0:T(8,128)S(1)} %get-tuple-element.24.divisor_ref, bf16[768,1024]{1,0:T(8,128)(2,1)S(1)} %copy-done.2, ...), custom_call_target="tpu_custom_call" | custom-call | flops 1207959552 | bytes 6291456 | tf_op jit(solution)/shard_map/pallas_call | solution.py:28
  (31 shorter events, 0.3 us)
Async XLA Ops:
  0.0 0.9 copy-start.6
  0.9 0.7 copy-start.8
  1.9 39.5 %collective-permute-start = (bf16[128,768]{1,0:T(8,128)(2,1)S(1)}, bf16[128,768]{1,0:T(8,128)(2,1)}, u32[]{:S(2)}, u32[]{:S(2)}) collective-permute-start(bf16[128,768]{1,0:T(8,128)(2,1)S(1)} %shard_map.129), channel_id=1, source_target_pairs={{0,16},{1,17},{34,50},{35,51},{64,80},{65,81},{98,114},{99,115},{1... | collective-permute-start | bytes 589832 | tf_op jit(solution)/shard_map/ppermute | solution.py:204
  21.9 19.5 %collective-permute-start.1 = (bf16[128,768]{1,0:T(8,128)(2,1)S(1)}, bf16[128,768]{1,0:T(8,128)(2,1)}, u32[]{:S(2)}, u32[]{:S(2)}) collective-permute-start(bf16[128,768]{1,0:T(8,128)(2,1)S(1)} %shard_map.129), channel_id=1, source_target_pairs={{16,0},{17,1},{50,34},{51,35},{80,64},{81,65},{114,98},{115,99},{1... | collective-permute-start | bytes 589832 | tf_op jit(solution)/shard_map/ppermute | solution.py:204
  23.2 0.7 copy-start.9
  23.9 0.7 copy-start.13
  24.6 0.7 copy-start.14
  26.4 16.9 %all-to-all-start = ((s32[32,1,128]{2,1,0:T(1,128)}), s32[32,1,128]{2,1,0:T(1,128)S(1)}, u32[]{:S(2)}, u32[]{:S(2)}) async-start(s32[32,1,128]{2,1,0:T(1,128)} %get-tuple-element.17), calls=%async_computation | async-start | bytes 32768 | tf_op jit(solution)/shard_map/all_to_all | solution.py:243
  34.0 1.9 %copy-start = (bf16[2048,768]{1,0:T(8,128)(2,1)S(1)}, bf16[2048,768]{1,0:T(8,128)(2,1)}, u32[]{:S(2)}) copy-start(bf16[2048,768]{1,0:T(8,128)(2,1)} %vals_ref.3) | copy-start | bytes 9437188
  35.9 0.8 copy-start.7
  46.8 1.2 copy-start.1
  47.9 9.9 %copy-start.16 = (bf16[128,768]{1,0:T(8,128)(2,1)S(1)}, bf16[128,768]{1,0:T(8,128)(2,1)}, u32[]{:S(2)}) copy-start(bf16[128,768]{1,0:T(8,128)(2,1)} %get-tuple-element.20) | copy-start | bytes 589828
  47.9 25.2 %copy-start.15 = (bf16[128,768]{1,0:T(8,128)(2,1)S(1)}, bf16[128,768]{1,0:T(8,128)(2,1)}, u32[]{:S(2)}) copy-start(bf16[128,768]{1,0:T(8,128)(2,1)} %get-tuple-element.19) | copy-start | bytes 589828
  47.9 47.4 %all-to-all-start.1 = ((bf16[32,32,768]{2,1,0:T(8,128)(2,1)}), bf16[32,32,768]{2,1,0:T(8,128)(2,1)S(1)}, u32[]{:S(2)}, u32[]{:S(2)}) async-start(bf16[32,32,768]{2,1,0:T(8,128)(2,1)} %bitcast.21), calls=%async_computation.1 | async-start | bytes 3145728 | tf_op jit(solution)/shard_map/all_to_all | solution.py:254
  57.9 19.3 %collective-permute-start.6 = (bf16[128,768]{1,0:T(8,128)(2,1)S(1)}, bf16[128,768]{1,0:T(8,128)(2,1)S(1)}, u32[]{:S(2)}, u32[]{:S(2)}) collective-permute-start(bf16[128,768]{1,0:T(8,128)(2,1)S(1)} %copy-done.16), channel_id=1, source_target_pairs={{0,24},{1,25},{16,8},{17,9},{34,58},{35,59},{50,42},{51,43},{64,88... | collective-permute-start | bytes 589832 | tf_op jit(solution)/shard_map/ppermute | solution.py:204
  73.1 5.5 %collective-permute-start.2 = (bf16[128,768]{1,0:T(8,128)(2,1)S(1)}, bf16[128,768]{1,0:T(8,128)(2,1)S(1)}, u32[]{:S(2)}, u32[]{:S(2)}) collective-permute-start(bf16[128,768]{1,0:T(8,128)(2,1)S(1)} %copy-done.15), channel_id=1, source_target_pairs={{0,8},{1,9},{16,24},{17,25},{34,42},{35,43},{50,58},{51,59},{64,72... | collective-permute-start | bytes 589832 | tf_op jit(solution)/shard_map/ppermute | solution.py:204
  77.3 6.1 %collective-permute-start.7 = (bf16[128,768]{1,0:T(8,128)(2,1)S(1)}, bf16[128,768]{1,0:T(8,128)(2,1)S(1)}, u32[]{:S(2)}, u32[]{:S(2)}) collective-permute-start(bf16[128,768]{1,0:T(8,128)(2,1)S(1)} %add.53), channel_id=1, source_target_pairs={{0,28},{1,29},{8,4},{9,5},{16,12},{17,13},{24,20},{25,21},{34,62},... | collective-permute-start | bytes 589832 | tf_op jit(solution)/shard_map/ppermute | solution.py:204
  78.6 6.1 %collective-permute-start.3 = (bf16[128,768]{1,0:T(8,128)(2,1)S(1)}, bf16[128,768]{1,0:T(8,128)(2,1)S(1)}, u32[]{:S(2)}, u32[]{:S(2)}) collective-permute-start(bf16[128,768]{1,0:T(8,128)(2,1)S(1)} %add.50), channel_id=1, source_target_pairs={{0,4},{1,5},{8,12},{9,13},{16,20},{17,21},{24,28},{25,29},{34,38},... | collective-permute-start | bytes 589832 | tf_op jit(solution)/shard_map/ppermute | solution.py:204
  83.4 4.5 %collective-permute-start.8 = (bf16[128,768]{1,0:T(8,128)(2,1)S(1)}, bf16[128,768]{1,0:T(8,128)(2,1)S(1)}, u32[]{:S(2)}, u32[]{:S(2)}) collective-permute-start(bf16[128,768]{1,0:T(8,128)(2,1)S(1)} %add.54), channel_id=1, source_target_pairs={{0,30},{1,31},{4,2},{5,3},{8,6},{9,7},{12,10},{13,11},{16,14},{17,... | collective-permute-start | bytes 589832 | tf_op jit(solution)/shard_map/ppermute | solution.py:204
  84.7 5.1 %collective-permute-start.4 = (bf16[128,768]{1,0:T(8,128)(2,1)S(1)}, bf16[128,768]{1,0:T(8,128)(2,1)S(1)}, u32[]{:S(2)}, u32[]{:S(2)}) collective-permute-start(bf16[128,768]{1,0:T(8,128)(2,1)S(1)} %add.51), channel_id=1, source_target_pairs={{0,2},{1,3},{4,6},{5,7},{8,10},{9,11},{12,14},{13,15},{16,18},{17,... | collective-permute-start | bytes 589832 | tf_op jit(solution)/shard_map/ppermute | solution.py:204
  87.9 4.4 %collective-permute-start.9 = (bf16[128,768]{1,0:T(8,128)(2,1)S(1)}, bf16[128,768]{1,0:T(8,128)(2,1)S(1)}, u32[]{:S(2)}, u32[]{:S(2)}) collective-permute-start(bf16[128,768]{1,0:T(8,128)(2,1)S(1)} %add.55.d_ref), channel_id=1, source_target_pairs={{0,1},{1,0},{2,3},{3,2},{4,5},{5,4},{6,7},{7,6},{8,9},{9,8},{10,11... | collective-permute-start | bytes 589832 | tf_op jit(solution)/shard_map/ppermute | solution.py:208
  89.9 3.5 %collective-permute-start.5 = (bf16[128,768]{1,0:T(8,128)(2,1)S(1)}, bf16[128,768]{1,0:T(8,128)(2,1)S(1)}, u32[]{:S(2)}, u32[]{:S(2)}) collective-permute-start(bf16[128,768]{1,0:T(8,128)(2,1)S(1)} %add.52.u_ref), channel_id=1, source_target_pairs={{0,1},{1,0},{2,3},{3,2},{4,5},{5,4},{6,7},{7,6},{8,9},{9,8},{10,11... | collective-permute-start | bytes 589832 | tf_op jit(solution)/shard_map/ppermute | solution.py:208
  93.3 11.2 %copy-start.17 = (s32[1,1,256,15]{2,1,3,0:T(1,128)S(1)}, s32[1,1,256,15]{2,1,3,0:T(1,128)}, u32[]{:S(2)}) copy-start(s32[1,1,256,15]{2,1,3,0:T(1,128)} %param.21) | copy-start | bytes 46084
  93.3 11.2 %copy-start.11 = (s32[1,1,256]{2,1,0:T(1,128)S(1)}, s32[1,1,256]{2,1,0:T(1,128)}, u32[]{:S(2)}) copy-start(s32[1,1,256]{2,1,0:T(1,128)} %param.20) | copy-start | bytes 3076
  93.3 11.2 %copy-start.12 = (s32[1,1,256]{2,1,0:T(1,128)S(1)}, s32[1,1,256]{2,1,0:T(1,128)}, u32[]{:S(2)}) copy-start(s32[1,1,256]{2,1,0:T(1,128)} %param.22) | copy-start | bytes 3076
  95.3 22.5 %all-to-all-start.2 = ((bf16[8,64,768]{2,1,0:T(8,128)(2,1)}), bf16[8,64,768]{2,1,0:T(8,128)(2,1)}, u32[]{:S(2)}, u32[]{:S(2)}) async-start(bf16[8,64,768]{2,1,0:T(8,128)(2,1)} %bitcast.12), calls=%async_computation.2 | async-start | bytes 1572864 | tf_op jit(solution)/shard_map/all_to_all | solution.py:288
  107.0 0.8 copy-start.4
  107.8 10.1 %copy-start.10 = (f32[1024]{0:T(1024)S(1)}, f32[1024]{0:T(1024)}, u32[]{:S(2)}) copy-start(f32[1024]{0:T(1024)} %param.25) | copy-start | bytes 12292
  117.8 1.4 %copy-start.2 = (bf16[768,1024]{1,0:T(8,128)(2,1)S(1)}, bf16[768,1024]{1,0:T(8,128)(2,1)}, u32[]{:S(2)}) copy-start(bf16[768,1024]{1,0:T(8,128)(2,1)} %w_self_ref.1) | copy-start | bytes 4718596
  119.2 1.4 %copy-start.3 = (bf16[768,1024]{1,0:T(8,128)(2,1)S(1)}, bf16[768,1024]{1,0:T(8,128)(2,1)}, u32[]{:S(2)}) copy-start(bf16[768,1024]{1,0:T(8,128)(2,1)} %w_nbr_ref.1) | copy-start | bytes 4718596
  120.6 1.0 copy-start.5

commit v2 on v1

v2 whole, which is shorter than its diff:
```python
import jax
import jax.numpy as jnp
from jax import lax
from jax.experimental import pallas as pl
from jax.experimental.pallas import tpu as pltpu
from jax.sharding import PartitionSpec as P

D = 768
F = 15
SB = 128
NB = 6
CAP = 32
HCAP = 16
FAR = (4, 12, 8)
LANES = 128
MIB = 1024 * 1024
F32 = jnp.float32
BF16 = jnp.bfloat16
I32 = jnp.int32


def iota(shape, axis):
    return lax.broadcasted_iota(I32, shape, axis)


def call(body, outs, ins, scalars=0, away=0, scratch=(), vmem=16, flops=0, moved=0):
    smem = pl.BlockSpec(memory_space=pltpu.SMEM)
    full = pl.BlockSpec(memory_space=pltpu.VMEM)
    hbm = pl.BlockSpec(memory_space=pltpu.HBM)
    many = isinstance(outs, (list, tuple))
    return pl.pallas_call(
        body,
        out_shape=outs,
        in_specs=[smem] * scalars + [hbm] * away + [full] * (len(ins) - scalars - away),
        out_specs=[full] * len(outs) if many else full,
        scratch_shapes=list(scratch),
        compiler_params=pltpu.CompilerParams(vmem_limit_bytes=vmem * MIB),
        cost_estimate=pl.CostEstimate(flops=flops, bytes_accessed=moved, transcendentals=0),
    )(*ins)


def fetch(pairs, sems):
    copies = [pltpu.make_async_copy(src, dst, sems.at[i]) for i, (src, dst) in enumerate(pairs)]
    for copy in copies:
        copy.start()
    return copies


def scale_terms(across):
    blank = jnp.zeros((8 - NB, LANES), F32)
    terms = []
    for _ in range(3):
        term = across.astype(BF16).astype(F32)
        across = across - term
        terms += [term, blank]
    terms.append(jnp.zeros((LANES - 24, LANES), F32))
    return jnp.concatenate(terms, axis=0).T.astype(BF16)


def dequantize_kernel(vals_ref, scales_ref, out_ref):
    term, feature = iota((LANES, D), 0), iota((LANES, D), 1)
    widen = ((term % 8 == feature // SB) & (term < 24)).astype(F32).astype(BF16)
    terms = [scale_terms(scales_ref[:, at : at + LANES]) for at in range(0, vals_ref.shape[0], LANES)]
    scales = jnp.dot(jnp.concatenate(terms, axis=0), widen, preferred_element_type=F32)
    out_ref[...] = (vals_ref[...].astype(F32) * scales).astype(BF16)


def dequantize(vals, scales):
    rows = vals.shape[0]
    return call(
        dequantize_kernel,
        jax.ShapeDtypeStruct((rows, D), BF16),
        [vals, scales.T],
        vmem=12,
        flops=rows * D,
        moved=rows * D * 4,
    )


def ask_kernel(cold_hbm, holder_hbm, slot_hbm, ask_ref, place_ref, cold_ref, holder_ref, slot_ref, sems):
    copies = fetch([(holder_hbm, holder_ref), (slot_hbm, slot_ref), (cold_hbm, cold_ref)], sems)
    for copy in copies:
        copy.wait()
    n = holder_ref.shape[1]
    across = jnp.broadcast_to(holder_ref[...], (n, n))
    down = across.T
    earlier = (across == down) & (iota((n, n), 1) < iota((n, n), 0))
    rank = jnp.sum(earlier.astype(F32), axis=1, keepdims=True).astype(I32)
    place_ref[...] = down[:, :LANES] * HCAP + rank
    owners = ask_ref.shape[0]
    named = jnp.broadcast_to(holder_ref[...], (owners, n)) == iota((owners, n), 0)
    slots = jnp.broadcast_to(slot_ref[...], (owners, n)).astype(F32)
    left = jnp.where(named, slots, 0.0).astype(BF16)
    right = (rank + CAP == iota((n, LANES), 1)).astype(F32).astype(BF16)
    hot = jnp.dot(left, right, preferred_element_type=F32).astype(I32)
    column = iota((1, LANES), 1)
    for p in range(owners):
        cold = cold_ref[:, (p // 4) * LANES : (p // 4 + 1) * LANES]
        if p % 4:
            cold = pltpu.roll(cold, LANES - CAP * (p % 4), 1)
        ask_ref[p] = jnp.where(column < CAP, cold, hot[p : p + 1])


def transposed(rows):
    n = rows.shape[0]
    if n < LANES:
        rows = jnp.concatenate([rows, jnp.zeros((LANES - n, LANES), I32)], axis=0)
    return rows.T


def pick(asks, first, group, at, count, source):
    rows = source.shape[0]
    return jnp.concatenate(
        [
            (asks[at : at + count, p : p + 1] == iota((count, rows), 1)).astype(F32).astype(BF16)
            for p in range(first, first + group)
        ],
        axis=0,
    )


def serve_cold_kernel(asked_ref, table_ref, out_ref):
    asks = transposed(jnp.concatenate([asked_ref[p] for p in range(32)], axis=0))
    group = 8
    for first in range(0, 32, group):
        mask = pick(asks, first, group, 0, CAP, table_ref)
        out_ref[first * CAP : (first + group) * CAP, :] = jnp.dot(
            mask, table_ref[...], preferred_element_type=F32
        ).astype(BF16)


def serve_hot_kernel(asked_ref, held_ref, out_ref):
    asks = transposed(jnp.concatenate([asked_ref[p] for p in range(32)], axis=0))
    mask = pick(asks, 0, 32, CAP, HCAP, held_ref)
    out_ref[...] = jnp.dot(mask, held_ref[...], preferred_element_type=F32).astype(BF16)


def weigh_kernel(self_ref, nbr_ref, count_ref, place_ref, cold_ref, hot_ref, divisor_ref):
    n = self_ref.shape[1]
    count = count_ref[...]
    own = self_ref[...]
    live = [jnp.where(count > f, nbr_ref[f], -1) for f in range(F)]

    def weights(at):
        position = iota((LANES, n), 0) + at * LANES
        picked = (own == position).astype(F32)
        times = jnp.zeros((LANES, n), F32)
        for f in range(F):
            times = times + (live[f] == position).astype(F32)
        return jnp.concatenate([picked.T, times.T], axis=0).astype(BF16)

    n_cold, slots = cold_ref.shape[1] // LANES, hot_ref.shape[1]
    for at in range(n_cold):
        cold_ref[:, at * LANES : (at + 1) * LANES] = weights(at)
    n_hot = place_ref.shape[0]
    hot = jnp.concatenate([weights(n_cold + at) for at in range(n_hot // LANES)], axis=1)
    place = jnp.concatenate([place_ref[...]] * (slots // LANES), axis=1)
    spread = (place == iota((n_hot, slots), 1)).astype(F32).astype(BF16)
    hot_ref[...] = jnp.dot(hot, spread, preferred_element_type=F32).astype(BF16)
    divisor = jnp.maximum(count, 1).astype(F32)
    divisor_ref[...] = jnp.broadcast_to(divisor, (LANES, n)).T


def cold_sum_kernel(w_self_hbm, w_nbr_hbm, weight_ref, rows_ref, weight_hot_ref, out_ref, w_ref, kept_ref, sems):
    copies = fetch([(w_self_hbm, w_ref.at[pl.ds(0, D)]), (w_nbr_hbm, w_ref.at[pl.ds(D, D)])], sems)
    out_ref[...] = jnp.dot(weight_ref[...], rows_ref[...], preferred_element_type=F32)
    kept_ref[...] = weight_hot_ref[...]
    for copy in copies:
        copy.wait()


def layer_kernel(part_ref, weight_ref, rows_ref, divisor_ref, w_ref, bias_ref, out_ref):
    n = out_ref.shape[0]
    total = part_ref[...] + jnp.dot(weight_ref[...], rows_ref[...], preferred_element_type=F32)
    own = total[:n].astype(BF16)
    divisor = jnp.concatenate([divisor_ref[...]] * (D // LANES), axis=1)
    mean = (total[n:] / divisor).astype(BF16)
    both = jnp.concatenate([own, mean], axis=1)
    mixed = jnp.dot(both, w_ref[...], preferred_element_type=F32) + bias_ref[...]
    out_ref[...] = jnp.maximum(mixed, 0.0).astype(BF16)


def send(array, starts, step):
    pairs = [
        (o * 32 + (o // 2 + s) % 16 * 2 + o % 2, o * 32 + (o // 2 + s + step) % 16 * 2 + o % 2)
        for o in range(32)
        for s in starts
    ]
    return lax.ppermute(array, ("owner", "replica"), pairs)


def across_chip(array):
    pairs = [(o * 32 + z * 2 + o % 2, o * 32 + z * 2 + 1 - o % 2) for o in range(32) for z in range(16)]
    return lax.ppermute(array, ("owner", "replica"), pairs)


def per_device(
    cold_vals,
    cold_scales,
    hot_vals,
    hot_scales,
    cold_req,
    hot_holder,
    hot_slot,
    self_pos,
    nbr_pos,
    nbr_count,
    w_self,
    w_nbr,
    bias,
):
    owner = lax.axis_index("owner")
    replica = lax.axis_index("replica")

    ask, place = call(
        ask_kernel,
        [jax.ShapeDtypeStruct((32, 1, LANES), I32), jax.ShapeDtypeStruct((256, LANES), I32)],
        [cold_req.reshape(1, 1024), hot_holder.reshape(1, 256), hot_slot.reshape(1, 256)],
        away=3,
        scratch=[
            pltpu.VMEM((1, 1024), I32),
            pltpu.VMEM((1, 256), I32),
            pltpu.VMEM((1, 256), I32),
            pltpu.SemaphoreType.DMA((3,)),
        ],
        vmem=60,
    )
    asked = lax.all_to_all(ask, "owner", split_axis=0, concat_axis=0, tiled=True)
    own = dequantize(hot_vals, hot_scales)
    asked, own = lax.optimization_barrier((asked, own))
    table = dequantize(cold_vals, cold_scales)
    served = call(
        serve_cold_kernel,
        jax.ShapeDtypeStruct((1024, D), BF16),
        [asked, table],
        vmem=12,
        flops=2 * 1024 * 2048 * D,
        moved=5 * MIB,
    )
    cold_rows = lax.all_to_all(served.reshape(32, CAP, D), "owner", split_axis=0, concat_axis=0, tiled=True)

    far = [send(own, (0,), step) for step in FAR]
    steps = (replica // 2 - owner // 2) % 16
    rows = jnp.where(steps == 0, own, sum(far[1:], far[0]))
    near = [send(rows, (0, *FAR), step) for step in (1, 15, 2)]
    rows = jnp.where(steps % 4 == 0, rows, sum(near[1:], near[0]))
    held = jnp.where(replica % 2 == owner % 2, rows, across_chip(rows))
    hot_served = call(
        serve_hot_kernel,
        jax.ShapeDtypeStruct((512, D), BF16),
        [asked, held],
        vmem=4,
        flops=2 * 512 * 128 * D,
        moved=2 * MIB,
    )
    hot_served, cold_rows = lax.optimization_barrier((hot_served, cold_rows))
    hot_rows = lax.all_to_all(hot_served.reshape(32, HCAP, D), "owner", split_axis=0, concat_axis=0, tiled=True)

    weight_cold, weight_hot, divisor = call(
        weigh_kernel,
        [
            jax.ShapeDtypeStruct((512, 1024), BF16),
            jax.ShapeDtypeStruct((512, 512), BF16),
            jax.ShapeDtypeStruct((256, LANES), F32),
        ],
        [
            self_pos.reshape(1, 256),
            jnp.transpose(nbr_pos.reshape(256, F)).reshape(F, 1, 256),
            nbr_count.reshape(1, 256),
            place,
        ],
        vmem=6,
        flops=16 * 512 * 1280,
        moved=2 * MIB,
    )
    part, weights, weight_hot = call(
        cold_sum_kernel,
        [
            jax.ShapeDtypeStruct((512, D), F32),
            jax.ShapeDtypeStruct((2 * D, 1024), BF16),
            jax.ShapeDtypeStruct((512, 512), BF16),
        ],
        [w_self, w_nbr, weight_cold, cold_rows.reshape(1024, D), weight_hot],
        away=2,
        scratch=[pltpu.SemaphoreType.DMA((2,))],
        vmem=6,
        flops=2 * 512 * 1024 * D,
        moved=8 * MIB,
    )
    hidden = call(
        layer_kernel,
        jax.ShapeDtypeStruct((256, 1024), BF16),
        [part, weight_hot, hot_rows.reshape(512, D), divisor, weights, bias.reshape(1, 1024)],
        vmem=8,
        flops=2 * 512 * 512 * D + 4 * 256 * D * 1024,
        moved=8 * MIB,
    )
    return hidden.reshape(1, 1, 256, 1024)


def solution(mesh):
    return jax.shard_map(
        per_device,
        mesh=mesh,
        in_specs=(
            P("owner", None),
            P("owner", None),
            P("replica", None),
            P("replica", None),
            P("owner", "replica", None),
            P("owner", "replica", None, None),
            P("owner", "replica", None),
            P("owner", "replica", None),
            P("owner", "replica", None, None),
            P("owner", "replica", None),
            P(),
            P(),
            P(),
        ),
        out_specs=P("owner", "replica", None, None),
        check_vma=False,
    )
```

time: 127 us -> 112 us (0.88)
  the two profiles are of different devices: /device:TPU:16 before, /device:TPU:8 now
where the time goes in v2:
time: 112 us
  waiting for transfers between devices  42.7 us (38%)
  starting transfers between devices  40.2 us (36%)
  local copies, waits for them, and re-layouts  14.5 us (13%)
  Pallas kernels  13.7 us (12%)
    ppermute x1, waiting for transfers between devices, across_chip(): return lax.ppermute(array, ('owner', 'replica'), pairs)  19.6 us
    all_to_all x1, starting transfers between devices, per_device(): lax.all_to_all(ask, 'owner', split_axis=0, concat_axis=0, tiled=True)  16.6 us
    unnamed x33, local copies, waits for them, and re-layouts  14.5 us
    all_to_all x1, waiting for transfers between devices, per_device(): lax.all_to_all(hot_served.reshape(32, HCAP, D), 'owner', split_axis=0, co...  14.2 us
    pallas_call x8, Pallas kernels, call(): pl.pallas_call(body, out_shape=outs, in_specs=[smem] * scalars + [hbm] *...  13.7 us
    all_to_all x1, starting transfers between devices, per_device(): lax.all_to_all(hot_served.reshape(32, HCAP, D), 'owner', split_axis=0, co...  11.4 us
    all_to_all x1, starting transfers between devices, per_device(): lax.all_to_all(served.reshape(32, CAP, D), 'owner', split_axis=0, concat_...  6.86 us
    all_to_all x1, waiting for transfers between devices, per_device(): lax.all_to_all(served.reshape(32, CAP, D), 'owner', split_axis=0, concat_...  5.86 us
  transfers between devices with their start and end apart: 10, of which 4 were waited for; matrix products, arithmetic and copies ran while one was open for 0% of the time, Pallas kernels for 6%

profile of v2, /device:TPU:8, one launch (start us, length us, event | category | flops | bytes accessed | tf_op | source)
XLA Modules:
  0.0 111.6 jit_solution(3362495390732325608)
XLA Ops:
  0.0 1.7 %shard_map.127 = (s32[32,1,128]{2,1,0:T(1,128)}, s32[256,128]{1,0:T(8,128)}) custom-call(s32[1,1024]{1,0:T(1,128)} %bitcast.27, s32[1,256]{1,0:T(1,128)} %bitcast.28, s32[1,256]{1,0:T(1,128)} %bitcast.29), custom_call_target="tpu_custom_call" | custom-call | tf_op jit(solution)/shard_map/pallas_call | solution.py:31
  1.7 16.6 %all-to-all-start = ((s32[32,1,128]{2,1,0:T(1,128)}), s32[32,1,128]{2,1,0:T(1,128)S(1)}, u32[]{:S(2)}, u32[]{:S(2)}) async-start(s32[32,1,128]{2,1,0:T(1,128)} %get-tuple-element.19), calls=%async_computation | async-start | bytes 32768 | tf_op jit(solution)/shard_map/all_to_all | solution.py:228
  18.3 0.0 copy-start.8
  18.3 0.9 copy-done.8
  19.2 0.7 copy-done.11
  19.9 0.3 shard_map.129
  20.2 0.0 copy-start
  20.2 1.9 %copy-done = bf16[2048,768]{1,0:T(8,128)(2,1)S(1)} copy-done((bf16[2048,768]{1,0:T(8,128)(2,1)S(1)}, bf16[2048,768]{1,0:T(8,128)(2,1)}, u32[]{:S(2)}) %copy-start) | copy-done | bytes 3145752
  22.1 0.8 copy-done.10
  22.9 1.0 shard_map.131.table_ref
  23.9 3.1 %all-to-all-done.asked_ref = s32[32,1,128]{2,1,0:T(1,128)S(1)} async-done(((s32[32,1,128]{2,1,0:T(1,128)}), s32[32,1,128]{2,1,0:T(1,128)S(1)}, u32[]{:S(2)}, u32[]{:S(2)}) %all-to-all-start) | async-done | bytes 16416 | tf_op jit(solution)/shard_map/all_to_all | solution.py:228
  27.0 3.5 %shard_map.132 = bf16[1024,768]{1,0:T(8,128)(2,1)S(1)} custom-call(s32[32,1,128]{2,1,0:T(1,128)S(1)} %all-to-all-done.asked_ref, bf16[2048,768]{1,0:T(8,128)(2,1)S(1)} %shard_map.131.table_ref), custom_call_target="tpu_custom_call" | custom-call | flops 3221225472 | bytes 5242880 | tf_op jit(solution)/shard_map/pallas_call | solution.py:31
  30.5 1.2 %copy-done.3 = bf16[1024,768]{1,0:T(8,128)(2,1)} copy-done((bf16[1024,768]{1,0:T(8,128)(2,1)}, bf16[1024,768]{1,0:T(8,128)(2,1)S(1)}, u32[]{:S(2)}) %copy-start.3) | copy-done | bytes 1572888
  31.7 6.9 %all-to-all-start.1 = ((bf16[32,32,768]{2,1,0:T(8,128)(2,1)}), bf16[32,32,768]{2,1,0:T(8,128)(2,1)S(1)}, u32[]{:S(2)}, u32[]{:S(2)}) async-start(bf16[32,32,768]{2,1,0:T(8,128)(2,1)} %bitcast.20), calls=%async_computation.1 | async-start | bytes 3145728 | tf_op jit(solution)/shard_map/all_to_all | solution.py:240
  38.6 0.7 collective-permute-start.2
  39.3 0.7 collective-permute-start.1
  39.9 0.7 collective-permute-start
  40.7 0.0 collective-permute-done.2
  40.7 0.0 collective-permute-done.1
  40.7 0.0 collective-permute-done
  40.8 0.7 collective-permute-start.5
  41.4 0.7 collective-permute-start.4
  42.1 0.7 collective-permute-start.3
  42.8 0.0 collective-permute-done.5
  42.8 0.0 collective-permute-done.4
  42.8 0.0 collective-permute-done.3
  42.9 1.3 %collective-permute-start.6 = (bf16[128,768]{1,0:T(8,128)(2,1)S(1)}, bf16[128,768]{1,0:T(8,128)(2,1)S(1)}, u32[]{:S(2)}, u32[]{:S(2)}) collective-permute-start(bf16[128,768]{1,0:T(8,128)(2,1)S(1)} %add_select_fusion), channel_id=1, source_target_pairs={{0,1},{2,3},{4,5},{6,7},{8,9},{10,11},{12,13},{14,15},{16,17},{18,... | collective-permute-start | bytes 589832 | tf_op jit(solution)/shard_map/ppermute | solution.py:194
  44.2 0.0 copy-start.15
  44.2 0.0 copy-start.9
  44.2 0.0 copy-start.13
  44.3 0.0 copy-start.14
  44.3 19.6 %collective-permute-done.6 = bf16[128,768]{1,0:T(8,128)(2,1)S(1)} collective-permute-done((bf16[128,768]{1,0:T(8,128)(2,1)S(1)}, bf16[128,768]{1,0:T(8,128)(2,1)S(1)}, u32[]{:S(2)}, u32[]{:S(2)}) %collective-permute-start.6) | collective-permute-done | bytes 196640 | tf_op jit(solution)/shard_map/ppermute | solution.py:194
  63.9 1.5 %shard_map.130 = bf16[512,768]{1,0:T(8,128)(2,1)} custom-call(s32[32,1,128]{2,1,0:T(1,128)S(1)} %all-to-all-done.asked_ref, bf16[128,768]{1,0:T(8,128)(2,1)S(1)} %broadcast_select_fusion.held_ref), custom_call_target="tpu_custom_call" | custom-call | flops 100663296 | bytes 2097152 | tf_op jit(solution)/shard_map/pallas_call | solution.py:31
  65.3 5.9 %all-to-all-done.1 = bf16[32,32,768]{2,1,0:T(8,128)(2,1)S(1)} async-done(((bf16[32,32,768]{2,1,0:T(8,128)(2,1)}), bf16[32,32,768]{2,1,0:T(8,128)(2,1)S(1)}, u32[]{:S(2)}, u32[]{:S(2)}) %all-to-all-start.1) | async-done | bytes 1572896 | tf_op jit(solution)/shard_map/all_to_all | solution.py:240
  71.2 11.4 %all-to-all-start.2 = ((bf16[32,16,768]{2,1,0:T(8,128)(2,1)}), bf16[32,16,768]{2,1,0:T(8,128)(2,1)S(1)}, u32[]{:S(2)}, u32[]{:S(2)}) async-start(bf16[32,16,768]{2,1,0:T(8,128)(2,1)} %bitcast.10), calls=%async_computation.2 | async-start | bytes 1572864 | tf_op jit(solution)/shard_map/all_to_all | solution.py:257
  82.6 0.0 copy-done.15
  82.6 0.0 copy-done.9
  82.7 2.4 %shard_map.128 = (bf16[512,1024]{1,0:T(8,128)(2,1)S(1)}, bf16[512,512]{1,0:T(8,128)(2,1)S(1)}, f32[256,128]{1,0:T(8,128)S(1)}) custom-call(s32[1,256]{1,0:T(1,128)S(1)} %bitcast.24, s32[15,1,256]{2,1,0:T(1,128)S(1)} %reshape.41.nbr_ref, s32[1,256]{1,0:T(1,128)S(1)} %bitcast.25, s32[256,128]{1,0:T(8,128)S(1)} %copy-done.9), custom_call_target="tpu_custom_call" | custom-call | flops 10485760 | bytes 2097152 | tf_op jit(solution)/shard_map/pallas_call | solution.py:31
  85.1 0.0 copy-start.4
  85.1 1.4 %copy-done.4 = bf16[768,1024]{1,0:T(8,128)(2,1)S(1)} copy-done((bf16[768,1024]{1,0:T(8,128)(2,1)S(1)}, bf16[768,1024]{1,0:T(8,128)(2,1)}, u32[]{:S(2)}) %copy-start.4) | copy-done | bytes 1572888
  86.5 1.4 %copy-done.5 = bf16[768,1024]{1,0:T(8,128)(2,1)S(1)} copy-done((bf16[768,1024]{1,0:T(8,128)(2,1)S(1)}, bf16[768,1024]{1,0:T(8,128)(2,1)}, u32[]{:S(2)}) %copy-start.5) | copy-done | bytes 1572888
  87.9 1.2 %shard_map.133 = (f32[512,768]{1,0:T(8,128)S(1)}, bf16[1536,1024]{1,0:T(8,128)(2,1)S(1)}, bf16[512,512]{1,0:T(8,128)(2,1)S(1)}) custom-call(bf16[768,1024]{1,0:T(8,128)(2,1)S(1)} %copy-done.4, bf16[768,1024]{1,0:T(8,128)(2,1)S(1)} %copy-done.5, bf16[512,1024]{1,0:T(8,128)(2,1)S(1)} %get-tuple-element.18.weight_ref, bf16[1024,768]{1,0:T(8,128)(2,1)S(1)} %bitcast.18, ...), custom_call_target="tpu_custom_call" | custom-call | flops 805306368 | bytes 8388608 | tf_op jit(solution)/shard_map/pallas_call | solution.py:31
  89.1 1.6 %copy-done.1 = bf16[1536,1024]{1,0:T(8,128)(2,1)} copy-done((bf16[1536,1024]{1,0:T(8,128)(2,1)}, bf16[1536,1024]{1,0:T(8,128)(2,1)S(1)}, u32[]{:S(2)}) %copy-start.1) | copy-done | bytes 3145752
  90.8 1.2 %copy-done.6 = f32[512,768]{1,0:T(8,128)} copy-done((f32[512,768]{1,0:T(8,128)}, f32[512,768]{1,0:T(8,128)S(1)}, u32[]{:S(2)}) %copy-start.6) | copy-done | bytes 1572888
  91.9 14.2 %all-to-all-done.2 = bf16[32,16,768]{2,1,0:T(8,128)(2,1)S(1)} async-done(((bf16[32,16,768]{2,1,0:T(8,128)(2,1)}), bf16[32,16,768]{2,1,0:T(8,128)(2,1)S(1)}, u32[]{:S(2)}, u32[]{:S(2)}) %all-to-all-start.2) | async-done | bytes 786464 | tf_op jit(solution)/shard_map/all_to_all | solution.py:257
  106.1 1.9 %copy-done.2 = bf16[1536,1024]{1,0:T(8,128)(2,1)S(1)} copy-done((bf16[1536,1024]{1,0:T(8,128)(2,1)S(1)}, bf16[1536,1024]{1,0:T(8,128)(2,1)}, u32[]{:S(2)}) %copy-start.2) | copy-done | bytes 3145752
  108.0 1.4 %copy-done.7 = f32[512,768]{1,0:T(8,128)S(1)} copy-done((f32[512,768]{1,0:T(8,128)S(1)}, f32[512,768]{1,0:T(8,128)}, u32[]{:S(2)}) %copy-start.7) | copy-done | bytes 1572888
  109.4 2.2 %shard_map.134 = bf16[256,1024]{1,0:T(8,128)(2,1)} custom-call(f32[512,768]{1,0:T(8,128)S(1)} %copy-done.7, bf16[512,512]{1,0:T(8,128)(2,1)S(1)} %get-tuple-element.25.weight_ref, bf16[512,768]{1,0:T(8,128)(2,1)S(1)} %bitcast.19, f32[256,128]{1,0:T(8,128)S(1)} %get-tuple-element.27.divisor_ref, bf16[1536,1024]{1,0:T(8,128)(2,1)S(1)} %copy-done.2, ...), custom_call_target="tpu_custom_call" | custom-call | flops 1207959552 | bytes 8388608 | tf_op jit(solution)/shard_map/pallas_call | solution.py:31
  (17 shorter events, 0.1 us)
Async XLA Ops:
  1.7 25.3 %all-to-all-start = ((s32[32,1,128]{2,1,0:T(1,128)}), s32[32,1,128]{2,1,0:T(1,128)S(1)}, u32[]{:S(2)}, u32[]{:S(2)}) async-start(s32[32,1,128]{2,1,0:T(1,128)} %get-tuple-element.19), calls=%async_computation | async-start | bytes 32768 | tf_op jit(solution)/shard_map/all_to_all | solution.py:228
  18.3 0.9 copy-start.8
  19.2 0.7 copy-start.11
  20.2 1.9 %copy-start = (bf16[2048,768]{1,0:T(8,128)(2,1)S(1)}, bf16[2048,768]{1,0:T(8,128)(2,1)}, u32[]{:S(2)}) copy-start(bf16[2048,768]{1,0:T(8,128)(2,1)} %vals_ref.3) | copy-start | bytes 9437188
  22.1 0.8 copy-start.10
  30.5 1.2 %copy-start.3 = (bf16[1024,768]{1,0:T(8,128)(2,1)}, bf16[1024,768]{1,0:T(8,128)(2,1)S(1)}, u32[]{:S(2)}) copy-start(bf16[1024,768]{1,0:T(8,128)(2,1)S(1)} %shard_map.132) | copy-start | bytes 4718596
  31.7 39.5 %all-to-all-start.1 = ((bf16[32,32,768]{2,1,0:T(8,128)(2,1)}), bf16[32,32,768]{2,1,0:T(8,128)(2,1)S(1)}, u32[]{:S(2)}, u32[]{:S(2)}) async-start(bf16[32,32,768]{2,1,0:T(8,128)(2,1)} %bitcast.20), calls=%async_computation.1 | async-start | bytes 3145728 | tf_op jit(solution)/shard_map/all_to_all | solution.py:240
  38.6 2.1 %collective-permute-start.2 = (bf16[128,768]{1,0:T(8,128)(2,1)S(1)}, bf16[128,768]{1,0:T(8,128)(2,1)S(1)}, u32[]{:S(2)}, u32[]{:S(2)}) collective-permute-start(bf16[128,768]{1,0:T(8,128)(2,1)S(1)} %shard_map.129), channel_id=1, source_target_pairs={{0,16},{33,49},{66,82},{99,115},{132,148},{165,181},{198,214},{231... | collective-permute-start | bytes 589832 | tf_op jit(solution)/shard_map/ppermute | solution.py:189
  39.3 1.4 %collective-permute-start.1 = (bf16[128,768]{1,0:T(8,128)(2,1)S(1)}, bf16[128,768]{1,0:T(8,128)(2,1)S(1)}, u32[]{:S(2)}, u32[]{:S(2)}) collective-permute-start(bf16[128,768]{1,0:T(8,128)(2,1)S(1)} %shard_map.129), channel_id=1, source_target_pairs={{0,24},{33,57},{66,90},{99,123},{132,156},{165,189},{198,222},{231... | collective-permute-start | bytes 589832 | tf_op jit(solution)/shard_map/ppermute | solution.py:189
  39.9 0.7 collective-permute-start
  40.8 2.1 %collective-permute-start.5 = (bf16[128,768]{1,0:T(8,128)(2,1)S(1)}, bf16[128,768]{1,0:T(8,128)(2,1)S(1)}, u32[]{:S(2)}, u32[]{:S(2)}) collective-permute-start(bf16[128,768]{1,0:T(8,128)(2,1)S(1)} %add_select_fusion.1), channel_id=1, source_target_pairs={{0,4},{8,12},{24,28},{16,20},{33,37},{41,45},{57,61},{49,53},{66,7... | collective-permute-start | bytes 589832 | tf_op jit(solution)/shard_map/ppermute | solution.py:189
  41.4 1.4 %collective-permute-start.4 = (bf16[128,768]{1,0:T(8,128)(2,1)S(1)}, bf16[128,768]{1,0:T(8,128)(2,1)S(1)}, u32[]{:S(2)}, u32[]{:S(2)}) collective-permute-start(bf16[128,768]{1,0:T(8,128)(2,1)S(1)} %add_select_fusion.1), channel_id=1, source_target_pairs={{0,30},{8,6},{24,22},{16,14},{33,63},{41,39},{57,55},{49,47},{66,6... | collective-permute-start | bytes 589832 | tf_op jit(solution)/shard_map/ppermute | solution.py:189
  42.1 0.7 collective-permute-start.3
  42.9 21.0 %collective-permute-start.6 = (bf16[128,768]{1,0:T(8,128)(2,1)S(1)}, bf16[128,768]{1,0:T(8,128)(2,1)S(1)}, u32[]{:S(2)}, u32[]{:S(2)}) collective-permute-start(bf16[128,768]{1,0:T(8,128)(2,1)S(1)} %add_select_fusion), channel_id=1, source_target_pairs={{0,1},{2,3},{4,5},{6,7},{8,9},{10,11},{12,13},{14,15},{16,17},{18,... | collective-permute-start | bytes 589832 | tf_op jit(solution)/shard_map/ppermute | solution.py:194
  44.2 38.4 %copy-start.15 = (s32[1,1,256,15]{2,1,3,0:T(1,128)S(1)}, s32[1,1,256,15]{2,1,3,0:T(1,128)}, u32[]{:S(2)}) copy-start(s32[1,1,256,15]{2,1,3,0:T(1,128)} %param.21) | copy-start | bytes 46084
  44.2 38.4 %copy-start.9 = (s32[256,128]{1,0:T(8,128)S(1)}, s32[256,128]{1,0:T(8,128)}, u32[]{:S(2)}) copy-start(s32[256,128]{1,0:T(8,128)} %get-tuple-element.17.place_ref) | copy-start | bytes 393220
  44.2 38.4 %copy-start.13 = (s32[1,1,256]{2,1,0:T(1,128)S(1)}, s32[1,1,256]{2,1,0:T(1,128)}, u32[]{:S(2)}) copy-start(s32[1,1,256]{2,1,0:T(1,128)} %param.20) | copy-start | bytes 3076
  44.3 38.4 %copy-start.14 = (s32[1,1,256]{2,1,0:T(1,128)S(1)}, s32[1,1,256]{2,1,0:T(1,128)}, u32[]{:S(2)}) copy-start(s32[1,1,256]{2,1,0:T(1,128)} %param.22) | copy-start | bytes 3076
  71.2 34.9 %all-to-all-start.2 = ((bf16[32,16,768]{2,1,0:T(8,128)(2,1)}), bf16[32,16,768]{2,1,0:T(8,128)(2,1)S(1)}, u32[]{:S(2)}, u32[]{:S(2)}) async-start(bf16[32,16,768]{2,1,0:T(8,128)(2,1)} %bitcast.10), calls=%async_computation.2 | async-start | bytes 1572864 | tf_op jit(solution)/shard_map/all_to_all | solution.py:257
  85.1 1.4 %copy-start.4 = (bf16[768,1024]{1,0:T(8,128)(2,1)S(1)}, bf16[768,1024]{1,0:T(8,128)(2,1)}, u32[]{:S(2)}) copy-start(bf16[768,1024]{1,0:T(8,128)(2,1)} %w_self_hbm.1) | copy-start | bytes 4718596
  86.5 1.4 %copy-start.5 = (bf16[768,1024]{1,0:T(8,128)(2,1)S(1)}, bf16[768,1024]{1,0:T(8,128)(2,1)}, u32[]{:S(2)}) copy-start(bf16[768,1024]{1,0:T(8,128)(2,1)} %w_nbr_hbm.1) | copy-start | bytes 4718596
  87.9 18.2 %copy-start.12 = (f32[1024]{0:T(1024)S(1)}, f32[1024]{0:T(1024)}, u32[]{:S(2)}) copy-start(f32[1024]{0:T(1024)} %param.25) | copy-start | bytes 12292
  89.1 1.6 %copy-start.1 = (bf16[1536,1024]{1,0:T(8,128)(2,1)}, bf16[1536,1024]{1,0:T(8,128)(2,1)S(1)}, u32[]{:S(2)}) copy-start(bf16[1536,1024]{1,0:T(8,128)(2,1)S(1)} %get-tuple-element.28.w_ref) | copy-start | bytes 9437188
  90.7 1.2 %copy-start.6 = (f32[512,768]{1,0:T(8,128)}, f32[512,768]{1,0:T(8,128)S(1)}, u32[]{:S(2)}) copy-start(f32[512,768]{1,0:T(8,128)S(1)} %get-tuple-element.24.part_ref) | copy-start | bytes 4718596
  106.1 1.9 %copy-start.2 = (bf16[1536,1024]{1,0:T(8,128)(2,1)S(1)}, bf16[1536,1024]{1,0:T(8,128)(2,1)}, u32[]{:S(2)}) copy-start(bf16[1536,1024]{1,0:T(8,128)(2,1)} %copy-done.1) | copy-start | bytes 9437188
  108.0 1.4 %copy-start.7 = (f32[512,768]{1,0:T(8,128)S(1)}, f32[512,768]{1,0:T(8,128)}, u32[]{:S(2)}) copy-start(f32[512,768]{1,0:T(8,128)} %copy-done.6) | copy-start | bytes 4718596

commit v3 on v2

--- a/solution.py
+++ b/solution.py
@@ -11,7 +11,6 @@
 NB = 6
 CAP = 32
 HCAP = 16
-FAR = (4, 12, 8)
 LANES = 128
 MIB = 1024 * 1024
 F32 = jnp.float32
@@ -180,11 +179,19 @@
     out_ref[...] = jnp.maximum(mixed, 0.0).astype(BF16)
 
 
-def send(array, starts, step):
+def relays(home):
+    place = min(home % 4, 2)
+    return [b * 4 + place for b in range(4) if b != home // 4]
+
+
+def onward(z):
+    steps = {0: (1, 2, -1), 1: (-1, 1, 2), 2: (-2, -1, 1), 3: (-3, -2, -1)}
+    return [(z + step) % 16 for step in steps[z % 4]]
+
+
+def down_columns(array, edges):
     pairs = [
-        (o * 32 + (o // 2 + s) % 16 * 2 + o % 2, o * 32 + (o // 2 + s + step) % 16 * 2 + o % 2)
-        for o in range(32)
-        for s in starts
+        (o * 32 + z * 2 + o % 2, o * 32 + there * 2 + o % 2) for o in range(32) for z, there in edges(o // 2)
     ]
     return lax.ppermute(array, ("owner", "replica"), pairs)
 
@@ -239,11 +246,15 @@
     )
     cold_rows = lax.all_to_all(served.reshape(32, CAP, D), "owner", split_axis=0, concat_axis=0, tiled=True)
 
-    far = [send(own, (0,), step) for step in FAR]
-    steps = (replica // 2 - owner // 2) % 16
-    rows = jnp.where(steps == 0, own, sum(far[1:], far[0]))
-    near = [send(rows, (0, *FAR), step) for step in (1, 15, 2)]
-    rows = jnp.where(steps % 4 == 0, rows, sum(near[1:], near[0]))
+    z, home = replica // 2, owner // 2
+    far = [down_columns(own, lambda h, turn=turn: [(h, relays(h)[turn])]) for turn in (2, 1, 0)]
+    rows = jnp.where(z == home, own, far[0] + far[1] + far[2])
+    beside = [down_columns(own, lambda h, turn=turn: [(h, onward(h)[turn])]) for turn in range(3)]
+    near = [
+        down_columns(rows, lambda h, turn=turn: [(at, onward(at)[turn]) for at in relays(h)]) for turn in range(3)
+    ]
+    relay = (z == home) | ((z // 4 != home // 4) & (z % 4 == jnp.minimum(home % 4, 2)))
+    rows = jnp.where(relay, rows, sum(beside[1:] + near, beside[0]))
     held = jnp.where(replica % 2 == owner % 2, rows, across_chip(rows))
     hot_served = call(
         serve_hot_kernel,

time: 112 us -> 109 us (0.973)
  waiting for transfers between devices: 42.7 us -> 40.6 us
    ppermute x1, waiting for transfers between devices: 19.6 us -> 15.1 us  [across_chip(): return lax.ppermute(array, ('owner', 'replica'), pairs)]
    all_to_all x1, starting transfers between devices: 11.4 us -> 8.38 us  [per_device(): lax.all_to_all(hot_served.reshape(32, HCAP, D), 'owner', split_axis=0, co...]
    all_to_all x1, waiting for transfers between devices: 5.86 us -> 8.24 us  [per_device(): lax.all_to_all(served.reshape(32, CAP, D), 'owner', split_axis=0, concat_...]
    ppermute x6 -> x9, starting transfers between devices: 4.04 us -> 6.06 us  [down_columns(): return lax.ppermute(array, ('owner', 'replica'), pairs)]
  transfers between devices with their start and end apart: 10 -> 13, of which waited for: 4 -> 4; matrix products, arithmetic and copies ran while one was open for 0% -> 0% of each run, Pallas kernels for 6% -> 6%
where the time goes in v3:
time: 109 us
  waiting for transfers between devices  40.6 us (37%)
  starting transfers between devices  39.1 us (36%)
  local copies, waits for them, and re-layouts  14.4 us (13%)
  Pallas kernels  13.7 us (13%)
    all_to_all x1, starting transfers between devices, per_device(): lax.all_to_all(ask, 'owner', split_axis=0, concat_axis=0, tiled=True)  16.6 us
    ppermute x1, waiting for transfers between devices, across_chip(): return lax.ppermute(array, ('owner', 'replica'), pairs)  15.1 us
    unnamed x33, local copies, waits for them, and re-layouts  14.4 us
    all_to_all x1, waiting for transfers between devices, per_device(): lax.all_to_all(hot_served.reshape(32, HCAP, D), 'owner', split_axis=0, co...  14.2 us
    pallas_call x8, Pallas kernels, call(): pl.pallas_call(body, out_shape=outs, in_specs=[smem] * scalars + [hbm] *...  13.7 us
    all_to_all x1, starting transfers between devices, per_device(): lax.all_to_all(hot_served.reshape(32, HCAP, D), 'owner', split_axis=0, co...  8.38 us
    all_to_all x1, waiting for transfers between devices, per_device(): lax.all_to_all(served.reshape(32, CAP, D), 'owner', split_axis=0, concat_...  8.24 us
    all_to_all x1, starting transfers between devices, per_device(): lax.all_to_all(served.reshape(32, CAP, D), 'owner', split_axis=0, concat_...  6.85 us
  transfers between devices with their start and end apart: 13, of which 4 were waited for; matrix products, arithmetic and copies ran while one was open for 0% of the time, Pallas kernels for 6%

profile of v3, /device:TPU:8, one launch (start us, length us, event | category | flops | bytes accessed | tf_op | source)
XLA Modules:
  0.0 108.6 jit_solution(16780221636185181518)
XLA Ops:
  0.0 1.7 %shard_map.127 = (s32[32,1,128]{2,1,0:T(1,128)}, s32[256,128]{1,0:T(8,128)}) custom-call(s32[1,1024]{1,0:T(1,128)} %bitcast.27, s32[1,256]{1,0:T(1,128)} %bitcast.28, s32[1,256]{1,0:T(1,128)} %bitcast.29), custom_call_target="tpu_custom_call" | custom-call | tf_op jit(solution)/shard_map/pallas_call | solution.py:30
  1.7 16.6 %all-to-all-start = ((s32[32,1,128]{2,1,0:T(1,128)}), s32[32,1,128]{2,1,0:T(1,128)S(1)}, u32[]{:S(2)}, u32[]{:S(2)}) async-start(s32[32,1,128]{2,1,0:T(1,128)} %get-tuple-element.19), calls=%async_computation | async-start | bytes 32768 | tf_op jit(solution)/shard_map/all_to_all | solution.py:235
  18.2 0.0 copy-start.8
  18.2 0.9 copy-done.8
  19.2 0.7 copy-done.11
  19.9 0.3 shard_map.129
  20.1 0.0 copy-start
  20.1 1.9 %copy-done = bf16[2048,768]{1,0:T(8,128)(2,1)S(1)} copy-done((bf16[2048,768]{1,0:T(8,128)(2,1)S(1)}, bf16[2048,768]{1,0:T(8,128)(2,1)}, u32[]{:S(2)}) %copy-start) | copy-done | bytes 3145752
  22.0 0.8 copy-done.10
  22.9 1.0 shard_map.131.table_ref
  23.9 3.1 %all-to-all-done.asked_ref = s32[32,1,128]{2,1,0:T(1,128)S(1)} async-done(((s32[32,1,128]{2,1,0:T(1,128)}), s32[32,1,128]{2,1,0:T(1,128)S(1)}, u32[]{:S(2)}, u32[]{:S(2)}) %all-to-all-start) | async-done | bytes 16416 | tf_op jit(solution)/shard_map/all_to_all | solution.py:235
  27.0 3.5 %shard_map.132 = bf16[1024,768]{1,0:T(8,128)(2,1)S(1)} custom-call(s32[32,1,128]{2,1,0:T(1,128)S(1)} %all-to-all-done.asked_ref, bf16[2048,768]{1,0:T(8,128)(2,1)S(1)} %shard_map.131.table_ref), custom_call_target="tpu_custom_call" | custom-call | flops 3221225472 | bytes 5242880 | tf_op jit(solution)/shard_map/pallas_call | solution.py:30
  30.5 1.2 %copy-done.3 = bf16[1024,768]{1,0:T(8,128)(2,1)} copy-done((bf16[1024,768]{1,0:T(8,128)(2,1)}, bf16[1024,768]{1,0:T(8,128)(2,1)S(1)}, u32[]{:S(2)}) %copy-start.3) | copy-done | bytes 1572888
  31.7 6.8 %all-to-all-start.1 = ((bf16[32,32,768]{2,1,0:T(8,128)(2,1)}), bf16[32,32,768]{2,1,0:T(8,128)(2,1)S(1)}, u32[]{:S(2)}, u32[]{:S(2)}) async-start(bf16[32,32,768]{2,1,0:T(8,128)(2,1)} %bitcast.20), calls=%async_computation.1 | async-start | bytes 3145728 | tf_op jit(solution)/shard_map/all_to_all | solution.py:247
  38.5 0.7 collective-permute-start.2
  39.2 0.7 collective-permute-start.1
  39.9 0.7 collective-permute-start
  40.6 0.7 collective-permute-start.5
  41.3 0.7 collective-permute-start.4
  42.0 0.7 collective-permute-start.3
  42.7 0.0 collective-permute-done
  42.7 0.7 collective-permute-start.8
  43.4 0.7 collective-permute-start.7
  44.1 0.0 collective-permute-done.5
  44.1 0.7 collective-permute-start.6
  44.8 0.0 collective-permute-done.4
  44.9 0.0 collective-permute-done.3
  44.9 0.1 add_select_fusion
  45.0 1.3 %collective-permute-start.9 = (bf16[128,768]{1,0:T(8,128)(2,1)S(1)}, bf16[128,768]{1,0:T(8,128)(2,1)S(1)}, u32[]{:S(2)}, u32[]{:S(2)}) collective-permute-start(bf16[128,768]{1,0:T(8,128)(2,1)S(1)} %add_select_fusion), channel_id=1, source_target_pairs={{0,1},{2,3},{4,5},{6,7},{8,9},{10,11},{12,13},{14,15},{16,17},{18,... | collective-permute-start | bytes 589832 | tf_op jit(solution)/shard_map/ppermute | solution.py:201
  46.3 0.0 copy-start.15
  46.3 0.0 copy-start.9
  46.3 0.0 copy-start.13
  46.3 0.0 copy-start.14
  46.3 15.1 %collective-permute-done.9 = bf16[128,768]{1,0:T(8,128)(2,1)S(1)} collective-permute-done((bf16[128,768]{1,0:T(8,128)(2,1)S(1)}, bf16[128,768]{1,0:T(8,128)(2,1)S(1)}, u32[]{:S(2)}, u32[]{:S(2)}) %collective-permute-start.9) | collective-permute-done | bytes 196640 | tf_op jit(solution)/shard_map/ppermute | solution.py:201
  61.5 1.5 %shard_map.130 = bf16[512,768]{1,0:T(8,128)(2,1)} custom-call(s32[32,1,128]{2,1,0:T(1,128)S(1)} %all-to-all-done.asked_ref, bf16[128,768]{1,0:T(8,128)(2,1)S(1)} %broadcast_select_fusion.held_ref), custom_call_target="tpu_custom_call" | custom-call | flops 100663296 | bytes 2097152 | tf_op jit(solution)/shard_map/pallas_call | solution.py:30
  62.9 8.2 %all-to-all-done.1 = bf16[32,32,768]{2,1,0:T(8,128)(2,1)S(1)} async-done(((bf16[32,32,768]{2,1,0:T(8,128)(2,1)}), bf16[32,32,768]{2,1,0:T(8,128)(2,1)S(1)}, u32[]{:S(2)}, u32[]{:S(2)}) %all-to-all-start.1) | async-done | bytes 1572896 | tf_op jit(solution)/shard_map/all_to_all | solution.py:247
  71.2 8.4 %all-to-all-start.2 = ((bf16[32,16,768]{2,1,0:T(8,128)(2,1)}), bf16[32,16,768]{2,1,0:T(8,128)(2,1)S(1)}, u32[]{:S(2)}, u32[]{:S(2)}) async-start(bf16[32,16,768]{2,1,0:T(8,128)(2,1)} %bitcast.10), calls=%async_computation.2 | async-start | bytes 1572864 | tf_op jit(solution)/shard_map/all_to_all | solution.py:268
  79.7 2.4 %shard_map.128 = (bf16[512,1024]{1,0:T(8,128)(2,1)S(1)}, bf16[512,512]{1,0:T(8,128)(2,1)S(1)}, f32[256,128]{1,0:T(8,128)S(1)}) custom-call(s32[1,256]{1,0:T(1,128)S(1)} %bitcast.24, s32[15,1,256]{2,1,0:T(1,128)S(1)} %reshape.41.nbr_ref, s32[1,256]{1,0:T(1,128)S(1)} %bitcast.25, s32[256,128]{1,0:T(8,128)S(1)} %copy-done.9), custom_call_target="tpu_custom_call" | custom-call | flops 10485760 | bytes 2097152 | tf_op jit(solution)/shard_map/pallas_call | solution.py:30
  82.1 0.0 copy-start.4
  82.1 1.4 %copy-done.4 = bf16[768,1024]{1,0:T(8,128)(2,1)S(1)} copy-done((bf16[768,1024]{1,0:T(8,128)(2,1)S(1)}, bf16[768,1024]{1,0:T(8,128)(2,1)}, u32[]{:S(2)}) %copy-start.4) | copy-done | bytes 1572888
  83.5 1.4 %copy-done.5 = bf16[768,1024]{1,0:T(8,128)(2,1)S(1)} copy-done((bf16[768,1024]{1,0:T(8,128)(2,1)S(1)}, bf16[768,1024]{1,0:T(8,128)(2,1)}, u32[]{:S(2)}) %copy-start.5) | copy-done | bytes 1572888
  84.9 1.2 %shard_map.133 = (f32[512,768]{1,0:T(8,128)S(1)}, bf16[1536,1024]{1,0:T(8,128)(2,1)S(1)}, bf16[512,512]{1,0:T(8,128)(2,1)S(1)}) custom-call(bf16[768,1024]{1,0:T(8,128)(2,1)S(1)} %copy-done.4, bf16[768,1024]{1,0:T(8,128)(2,1)S(1)} %copy-done.5, bf16[512,1024]{1,0:T(8,128)(2,1)S(1)} %get-tuple-element.18.weight_ref, bf16[1024,768]{1,0:T(8,128)(2,1)S(1)} %bitcast.18, ...), custom_call_target="tpu_custom_call" | custom-call | flops 805306368 | bytes 8388608 | tf_op jit(solution)/shard_map/pallas_call | solution.py:30
  86.1 1.6 %copy-done.1 = bf16[1536,1024]{1,0:T(8,128)(2,1)} copy-done((bf16[1536,1024]{1,0:T(8,128)(2,1)}, bf16[1536,1024]{1,0:T(8,128)(2,1)S(1)}, u32[]{:S(2)}) %copy-start.1) | copy-done | bytes 3145752
  87.7 1.2 %copy-done.6 = f32[512,768]{1,0:T(8,128)} copy-done((f32[512,768]{1,0:T(8,128)}, f32[512,768]{1,0:T(8,128)S(1)}, u32[]{:S(2)}) %copy-start.6) | copy-done | bytes 1572888
  88.9 14.2 %all-to-all-done.2 = bf16[32,16,768]{2,1,0:T(8,128)(2,1)S(1)} async-done(((bf16[32,16,768]{2,1,0:T(8,128)(2,1)}), bf16[32,16,768]{2,1,0:T(8,128)(2,1)S(1)}, u32[]{:S(2)}, u32[]{:S(2)}) %all-to-all-start.2) | async-done | bytes 786464 | tf_op jit(solution)/shard_map/all_to_all | solution.py:268
  103.1 1.9 %copy-done.2 = bf16[1536,1024]{1,0:T(8,128)(2,1)S(1)} copy-done((bf16[1536,1024]{1,0:T(8,128)(2,1)S(1)}, bf16[1536,1024]{1,0:T(8,128)(2,1)}, u32[]{:S(2)}) %copy-start.2) | copy-done | bytes 3145752
  105.0 1.4 %copy-done.7 = f32[512,768]{1,0:T(8,128)S(1)} copy-done((f32[512,768]{1,0:T(8,128)S(1)}, f32[512,768]{1,0:T(8,128)}, u32[]{:S(2)}) %copy-start.7) | copy-done | bytes 1572888
  106.4 2.2 %shard_map.134 = bf16[256,1024]{1,0:T(8,128)(2,1)} custom-call(f32[512,768]{1,0:T(8,128)S(1)} %copy-done.7, bf16[512,512]{1,0:T(8,128)(2,1)S(1)} %get-tuple-element.25.weight_ref, bf16[512,768]{1,0:T(8,128)(2,1)S(1)} %bitcast.19, f32[256,128]{1,0:T(8,128)S(1)} %get-tuple-element.27.divisor_ref, bf16[1536,1024]{1,0:T(8,128)(2,1)S(1)} %copy-done.2, ...), custom_call_target="tpu_custom_call" | custom-call | flops 1207959552 | bytes 8388608 | tf_op jit(solution)/shard_map/pallas_call | solution.py:30
  (23 shorter events, 0.1 us)
Async XLA Ops:
  1.7 25.3 %all-to-all-start = ((s32[32,1,128]{2,1,0:T(1,128)}), s32[32,1,128]{2,1,0:T(1,128)S(1)}, u32[]{:S(2)}, u32[]{:S(2)}) async-start(s32[32,1,128]{2,1,0:T(1,128)} %get-tuple-element.19), calls=%async_computation | async-start | bytes 32768 | tf_op jit(solution)/shard_map/all_to_all | solution.py:235
  18.2 0.9 copy-start.8
  19.2 0.7 copy-start.11
  20.1 1.9 %copy-start = (bf16[2048,768]{1,0:T(8,128)(2,1)S(1)}, bf16[2048,768]{1,0:T(8,128)(2,1)}, u32[]{:S(2)}) copy-start(bf16[2048,768]{1,0:T(8,128)(2,1)} %vals_ref.3) | copy-start | bytes 9437188
  22.0 0.8 copy-start.10
  30.5 1.2 %copy-start.3 = (bf16[1024,768]{1,0:T(8,128)(2,1)}, bf16[1024,768]{1,0:T(8,128)(2,1)S(1)}, u32[]{:S(2)}) copy-start(bf16[1024,768]{1,0:T(8,128)(2,1)S(1)} %shard_map.132) | copy-start | bytes 4718596
  31.7 39.5 %all-to-all-start.1 = ((bf16[32,32,768]{2,1,0:T(8,128)(2,1)}), bf16[32,32,768]{2,1,0:T(8,128)(2,1)S(1)}, u32[]{:S(2)}, u32[]{:S(2)}) async-start(bf16[32,32,768]{2,1,0:T(8,128)(2,1)} %bitcast.20), calls=%async_computation.1 | async-start | bytes 3145728 | tf_op jit(solution)/shard_map/all_to_all | solution.py:247
  38.5 3.4 %collective-permute-start.2 = (bf16[128,768]{1,0:T(8,128)(2,1)S(1)}, bf16[128,768]{1,0:T(8,128)(2,1)S(1)}, u32[]{:S(2)}, u32[]{:S(2)}) collective-permute-start(bf16[128,768]{1,0:T(8,128)(2,1)S(1)} %shard_map.129), channel_id=1, source_target_pairs={{0,8},{33,41},{66,74},{99,107},{132,140},{165,173},{198,204},{231,... | collective-permute-start | bytes 589832 | tf_op jit(solution)/shard_map/ppermute | solution.py:196
  39.2 3.4 %collective-permute-start.1 = (bf16[128,768]{1,0:T(8,128)(2,1)S(1)}, bf16[128,768]{1,0:T(8,128)(2,1)S(1)}, u32[]{:S(2)}, u32[]{:S(2)}) collective-permute-start(bf16[128,768]{1,0:T(8,128)(2,1)S(1)} %shard_map.129), channel_id=1, source_target_pairs={{0,16},{33,49},{66,82},{99,115},{132,148},{165,181},{198,212},{231... | collective-permute-start | bytes 589832 | tf_op jit(solution)/shard_map/ppermute | solution.py:196
  39.9 2.8 %collective-permute-start = (bf16[128,768]{1,0:T(8,128)(2,1)S(1)}, bf16[128,768]{1,0:T(8,128)(2,1)S(1)}, u32[]{:S(2)}, u32[]{:S(2)}) collective-permute-start(bf16[128,768]{1,0:T(8,128)(2,1)S(1)} %shard_map.129), channel_id=1, source_target_pairs={{0,24},{33,57},{66,90},{99,123},{132,156},{165,189},{198,220},{231... | collective-permute-start | bytes 589832 | tf_op jit(solution)/shard_map/ppermute | solution.py:196
  40.6 3.5 %collective-permute-start.5 = (bf16[128,768]{1,0:T(8,128)(2,1)S(1)}, bf16[128,768]{1,0:T(8,128)(2,1)S(1)}, u32[]{:S(2)}, u32[]{:S(2)}) collective-permute-start(bf16[128,768]{1,0:T(8,128)(2,1)S(1)} %shard_map.129), channel_id=1, source_target_pairs={{0,30},{33,63},{66,70},{99,103},{132,134},{165,167},{198,196},{231... | collective-permute-start | bytes 589832 | tf_op jit(solution)/shard_map/ppermute | solution.py:196
  41.3 3.6 %collective-permute-start.4 = (bf16[128,768]{1,0:T(8,128)(2,1)S(1)}, bf16[128,768]{1,0:T(8,128)(2,1)S(1)}, u32[]{:S(2)}, u32[]{:S(2)}) collective-permute-start(bf16[128,768]{1,0:T(8,128)(2,1)S(1)} %shard_map.129), channel_id=1, source_target_pairs={{0,4},{33,37},{66,68},{99,101},{132,130},{165,163},{198,194},{231,... | collective-permute-start | bytes 589832 | tf_op jit(solution)/shard_map/ppermute | solution.py:196
  42.0 2.9 %collective-permute-start.3 = (bf16[128,768]{1,0:T(8,128)(2,1)S(1)}, bf16[128,768]{1,0:T(8,128)(2,1)S(1)}, u32[]{:S(2)}, u32[]{:S(2)}) collective-permute-start(bf16[128,768]{1,0:T(8,128)(2,1)S(1)} %shard_map.129), channel_id=1, source_target_pairs={{0,2},{33,35},{66,64},{99,97},{132,128},{165,161},{198,192},{231,2... | collective-permute-start | bytes 589832 | tf_op jit(solution)/shard_map/ppermute | solution.py:196
  42.7 2.1 %collective-permute-start.8 = (bf16[128,768]{1,0:T(8,128)(2,1)S(1)}, bf16[128,768]{1,0:T(8,128)(2,1)S(1)}, u32[]{:S(2)}, u32[]{:S(2)}) collective-permute-start(bf16[128,768]{1,0:T(8,128)(2,1)S(1)} %add_select_fusion.1), channel_id=1, source_target_pairs={{8,6},{16,14},{24,22},{41,39},{49,47},{57,55},{74,78},{82,86},{90,... | collective-permute-start | bytes 589832 | tf_op jit(solution)/shard_map/ppermute | solution.py:196
  43.4 1.5 %collective-permute-start.7 = (bf16[128,768]{1,0:T(8,128)(2,1)S(1)}, bf16[128,768]{1,0:T(8,128)(2,1)S(1)}, u32[]{:S(2)}, u32[]{:S(2)}) collective-permute-start(bf16[128,768]{1,0:T(8,128)(2,1)S(1)} %add_select_fusion.1), channel_id=1, source_target_pairs={{8,12},{16,20},{24,28},{41,45},{49,53},{57,61},{74,76},{82,84},{90... | collective-permute-start | bytes 589832 | tf_op jit(solution)/shard_map/ppermute | solution.py:196
  44.1 0.8 collective-permute-start.6
  45.0 16.5 %collective-permute-start.9 = (bf16[128,768]{1,0:T(8,128)(2,1)S(1)}, bf16[128,768]{1,0:T(8,128)(2,1)S(1)}, u32[]{:S(2)}, u32[]{:S(2)}) collective-permute-start(bf16[128,768]{1,0:T(8,128)(2,1)S(1)} %add_select_fusion), channel_id=1, source_target_pairs={{0,1},{2,3},{4,5},{6,7},{8,9},{10,11},{12,13},{14,15},{16,17},{18,... | collective-permute-start | bytes 589832 | tf_op jit(solution)/shard_map/ppermute | solution.py:201
  46.3 33.3 %copy-start.15 = (s32[1,1,256,15]{2,1,3,0:T(1,128)S(1)}, s32[1,1,256,15]{2,1,3,0:T(1,128)}, u32[]{:S(2)}) copy-start(s32[1,1,256,15]{2,1,3,0:T(1,128)} %param.21) | copy-start | bytes 46084
  46.3 33.3 %copy-start.9 = (s32[256,128]{1,0:T(8,128)S(1)}, s32[256,128]{1,0:T(8,128)}, u32[]{:S(2)}) copy-start(s32[256,128]{1,0:T(8,128)} %get-tuple-element.17.place_ref) | copy-start | bytes 393220
  46.3 33.3 %copy-start.13 = (s32[1,1,256]{2,1,0:T(1,128)S(1)}, s32[1,1,256]{2,1,0:T(1,128)}, u32[]{:S(2)}) copy-start(s32[1,1,256]{2,1,0:T(1,128)} %param.20) | copy-start | bytes 3076
  46.3 33.3 %copy-start.14 = (s32[1,1,256]{2,1,0:T(1,128)S(1)}, s32[1,1,256]{2,1,0:T(1,128)}, u32[]{:S(2)}) copy-start(s32[1,1,256]{2,1,0:T(1,128)} %param.22) | copy-start | bytes 3076
  71.2 31.9 %all-to-all-start.2 = ((bf16[32,16,768]{2,1,0:T(8,128)(2,1)}), bf16[32,16,768]{2,1,0:T(8,128)(2,1)S(1)}, u32[]{:S(2)}, u32[]{:S(2)}) async-start(bf16[32,16,768]{2,1,0:T(8,128)(2,1)} %bitcast.10), calls=%async_computation.2 | async-start | bytes 1572864 | tf_op jit(solution)/shard_map/all_to_all | solution.py:268
  82.1 1.4 %copy-start.4 = (bf16[768,1024]{1,0:T(8,128)(2,1)S(1)}, bf16[768,1024]{1,0:T(8,128)(2,1)}, u32[]{:S(2)}) copy-start(bf16[768,1024]{1,0:T(8,128)(2,1)} %w_self_hbm.1) | copy-start | bytes 4718596
  83.5 1.4 %copy-start.5 = (bf16[768,1024]{1,0:T(8,128)(2,1)S(1)}, bf16[768,1024]{1,0:T(8,128)(2,1)}, u32[]{:S(2)}) copy-start(bf16[768,1024]{1,0:T(8,128)(2,1)} %w_nbr_hbm.1) | copy-start | bytes 4718596
  84.9 18.2 %copy-start.12 = (f32[1024]{0:T(1024)S(1)}, f32[1024]{0:T(1024)}, u32[]{:S(2)}) copy-start(f32[1024]{0:T(1024)} %param.25) | copy-start | bytes 12292
  86.1 1.6 %copy-start.1 = (bf16[1536,1024]{1,0:T(8,128)(2,1)}, bf16[1536,1024]{1,0:T(8,128)(2,1)S(1)}, u32[]{:S(2)}) copy-start(bf16[1536,1024]{1,0:T(8,128)(2,1)S(1)} %get-tuple-element.28.w_ref) | copy-start | bytes 9437188
  87.7 1.2 %copy-start.6 = (f32[512,768]{1,0:T(8,128)}, f32[512,768]{1,0:T(8,128)S(1)}, u32[]{:S(2)}) copy-start(f32[512,768]{1,0:T(8,128)S(1)} %get-tuple-element.24.part_ref) | copy-start | bytes 4718596
  103.1 1.9 %copy-start.2 = (bf16[1536,1024]{1,0:T(8,128)(2,1)S(1)}, bf16[1536,1024]{1,0:T(8,128)(2,1)}, u32[]{:S(2)}) copy-start(bf16[1536,1024]{1,0:T(8,128)(2,1)} %copy-done.1) | copy-start | bytes 9437188
  105.0 1.4 %copy-start.7 = (f32[512,768]{1,0:T(8,128)S(1)}, f32[512,768]{1,0:T(8,128)}, u32[]{:S(2)}) copy-start(f32[512,768]{1,0:T(8,128)} %copy-done.6) | copy-start | bytes 4718596

commit v4 on v3

--- a/solution.py
+++ b/solution.py
@@ -249,9 +249,10 @@
     z, home = replica // 2, owner // 2
     far = [down_columns(own, lambda h, turn=turn: [(h, relays(h)[turn])]) for turn in (2, 1, 0)]
     rows = jnp.where(z == home, own, far[0] + far[1] + far[2])
-    beside = [down_columns(own, lambda h, turn=turn: [(h, onward(h)[turn])]) for turn in range(3)]
+    beside = [down_columns(own, lambda h, turn=turn: [(h, onward(h)[turn])]) for turn in (2, 1, 0)]
     near = [
-        down_columns(rows, lambda h, turn=turn: [(at, onward(at)[turn]) for at in relays(h)]) for turn in range(3)
+        down_columns(rows, lambda h, turn=turn: [(at, onward(at)[turn]) for at in relays(h)])
+        for turn in (2, 1, 0)
     ]
     relay = (z == home) | ((z // 4 != home // 4) & (z % 4 == jnp.minimum(home % 4, 2)))
     rows = jnp.where(relay, rows, sum(beside[1:] + near, beside[0]))

time: 109 us -> 106 us (0.972)
  starting transfers between devices: 39.1 us -> 36 us
    all_to_all x1, starting transfers between devices: 8.38 us -> 5.21 us  [per_device(): lax.all_to_all(hot_served.reshape(32, HCAP, D), 'owner', split_axis=0, co...]
where the time goes in v4:
time: 106 us; the launch traced here: 105 us
  waiting for transfers between devices  40.4 us (38%)
  starting transfers between devices  36 us (34%)
  local copies, waits for them, and re-layouts  14.4 us (14%)
  Pallas kernels  13.7 us (13%)
    all_to_all x1, starting transfers between devices, per_device(): lax.all_to_all(ask, 'owner', split_axis=0, concat_axis=0, tiled=True)  16.6 us
    unnamed x33, local copies, waits for them, and re-layouts  14.4 us
    ppermute x1, waiting for transfers between devices, across_chip(): return lax.ppermute(array, ('owner', 'replica'), pairs)  14.3 us
    all_to_all x1, waiting for transfers between devices, per_device(): lax.all_to_all(hot_served.reshape(32, HCAP, D), 'owner', split_axis=0, co...  14 us
    pallas_call x8, Pallas kernels, call(): pl.pallas_call(body, out_shape=outs, in_specs=[smem] * scalars + [hbm] *...  13.7 us
    all_to_all x1, waiting for transfers between devices, per_device(): lax.all_to_all(served.reshape(32, CAP, D), 'owner', split_axis=0, concat_...  9.03 us
    all_to_all x1, starting transfers between devices, per_device(): lax.all_to_all(served.reshape(32, CAP, D), 'owner', split_axis=0, concat_...  6.85 us
    ppermute x9, starting transfers between devices, down_columns(): return lax.ppermute(array, ('owner', 'replica'), pairs)  6.06 us
  transfers between devices with their start and end apart: 13, of which 4 were waited for; matrix products, arithmetic and copies ran while one was open for 0% of the time, Pallas kernels for 6%

profile of v4, /device:TPU:8, one launch (start us, length us, event | category | flops | bytes accessed | tf_op | source)
XLA Modules:
  0.0 105.2 jit_solution(1884204152838553981)
XLA Ops:
  0.0 1.7 %shard_map.127 = (s32[32,1,128]{2,1,0:T(1,128)}, s32[256,128]{1,0:T(8,128)}) custom-call(s32[1,1024]{1,0:T(1,128)} %bitcast.27, s32[1,256]{1,0:T(1,128)} %bitcast.28, s32[1,256]{1,0:T(1,128)} %bitcast.29), custom_call_target="tpu_custom_call" | custom-call | tf_op jit(solution)/shard_map/pallas_call | solution.py:30
  1.7 16.6 %all-to-all-start = ((s32[32,1,128]{2,1,0:T(1,128)}), s32[32,1,128]{2,1,0:T(1,128)S(1)}, u32[]{:S(2)}, u32[]{:S(2)}) async-start(s32[32,1,128]{2,1,0:T(1,128)} %get-tuple-element.19), calls=%async_computation | async-start | bytes 32768 | tf_op jit(solution)/shard_map/all_to_all | solution.py:235
  18.2 0.0 copy-start.8
  18.2 0.9 copy-done.8
  19.2 0.7 copy-done.11
  19.9 0.3 shard_map.129
  20.1 0.0 copy-start
  20.1 1.9 %copy-done = bf16[2048,768]{1,0:T(8,128)(2,1)S(1)} copy-done((bf16[2048,768]{1,0:T(8,128)(2,1)S(1)}, bf16[2048,768]{1,0:T(8,128)(2,1)}, u32[]{:S(2)}) %copy-start) | copy-done | bytes 3145752
  22.0 0.8 copy-done.10
  22.9 1.0 shard_map.131.table_ref
  23.9 3.1 %all-to-all-done.asked_ref = s32[32,1,128]{2,1,0:T(1,128)S(1)} async-done(((s32[32,1,128]{2,1,0:T(1,128)}), s32[32,1,128]{2,1,0:T(1,128)S(1)}, u32[]{:S(2)}, u32[]{:S(2)}) %all-to-all-start) | async-done | bytes 16416 | tf_op jit(solution)/shard_map/all_to_all | solution.py:235
  27.0 3.5 %shard_map.132 = bf16[1024,768]{1,0:T(8,128)(2,1)S(1)} custom-call(s32[32,1,128]{2,1,0:T(1,128)S(1)} %all-to-all-done.asked_ref, bf16[2048,768]{1,0:T(8,128)(2,1)S(1)} %shard_map.131.table_ref), custom_call_target="tpu_custom_call" | custom-call | flops 3221225472 | bytes 5242880 | tf_op jit(solution)/shard_map/pallas_call | solution.py:30
  30.5 1.2 %copy-done.3 = bf16[1024,768]{1,0:T(8,128)(2,1)} copy-done((bf16[1024,768]{1,0:T(8,128)(2,1)}, bf16[1024,768]{1,0:T(8,128)(2,1)S(1)}, u32[]{:S(2)}) %copy-start.3) | copy-done | bytes 1572888
  31.7 6.8 %all-to-all-start.1 = ((bf16[32,32,768]{2,1,0:T(8,128)(2,1)}), bf16[32,32,768]{2,1,0:T(8,128)(2,1)S(1)}, u32[]{:S(2)}, u32[]{:S(2)}) async-start(bf16[32,32,768]{2,1,0:T(8,128)(2,1)} %bitcast.20), calls=%async_computation.1 | async-start | bytes 3145728 | tf_op jit(solution)/shard_map/all_to_all | solution.py:247
  38.5 0.7 collective-permute-start.2
  39.2 0.7 collective-permute-start.1
  39.9 0.7 collective-permute-start
  40.6 0.7 collective-permute-start.5
  41.3 0.7 collective-permute-start.4
  42.0 0.7 collective-permute-start.3
  42.7 0.0 collective-permute-done
  42.7 0.7 collective-permute-start.8
  43.4 0.7 collective-permute-start.7
  44.1 0.0 collective-permute-done.5
  44.1 0.7 collective-permute-start.6
  44.8 0.0 collective-permute-done.4
  44.9 0.0 collective-permute-done.3
  44.9 0.1 add_select_fusion
  45.0 1.3 %collective-permute-start.9 = (bf16[128,768]{1,0:T(8,128)(2,1)S(1)}, bf16[128,768]{1,0:T(8,128)(2,1)S(1)}, u32[]{:S(2)}, u32[]{:S(2)}) collective-permute-start(bf16[128,768]{1,0:T(8,128)(2,1)S(1)} %add_select_fusion), channel_id=1, source_target_pairs={{0,1},{2,3},{4,5},{6,7},{8,9},{10,11},{12,13},{14,15},{16,17},{18,... | collective-permute-start | bytes 589832 | tf_op jit(solution)/shard_map/ppermute | solution.py:201
  46.3 0.0 copy-start.15
  46.3 0.0 copy-start.9
  46.3 0.0 copy-start.13
  46.3 0.0 copy-start.14
  46.3 14.3 %collective-permute-done.9 = bf16[128,768]{1,0:T(8,128)(2,1)S(1)} collective-permute-done((bf16[128,768]{1,0:T(8,128)(2,1)S(1)}, bf16[128,768]{1,0:T(8,128)(2,1)S(1)}, u32[]{:S(2)}, u32[]{:S(2)}) %collective-permute-start.9) | collective-permute-done | bytes 196640 | tf_op jit(solution)/shard_map/ppermute | solution.py:201
  60.7 1.5 %shard_map.130 = bf16[512,768]{1,0:T(8,128)(2,1)} custom-call(s32[32,1,128]{2,1,0:T(1,128)S(1)} %all-to-all-done.asked_ref, bf16[128,768]{1,0:T(8,128)(2,1)S(1)} %broadcast_select_fusion.held_ref), custom_call_target="tpu_custom_call" | custom-call | flops 100663296 | bytes 2097152 | tf_op jit(solution)/shard_map/pallas_call | solution.py:30
  62.2 9.0 %all-to-all-done.1 = bf16[32,32,768]{2,1,0:T(8,128)(2,1)S(1)} async-done(((bf16[32,32,768]{2,1,0:T(8,128)(2,1)}), bf16[32,32,768]{2,1,0:T(8,128)(2,1)S(1)}, u32[]{:S(2)}, u32[]{:S(2)}) %all-to-all-start.1) | async-done | bytes 1572896 | tf_op jit(solution)/shard_map/all_to_all | solution.py:247
  71.2 5.2 %all-to-all-start.2 = ((bf16[32,16,768]{2,1,0:T(8,128)(2,1)}), bf16[32,16,768]{2,1,0:T(8,128)(2,1)S(1)}, u32[]{:S(2)}, u32[]{:S(2)}) async-start(bf16[32,16,768]{2,1,0:T(8,128)(2,1)} %bitcast.10), calls=%async_computation.2 | async-start | bytes 1572864 | tf_op jit(solution)/shard_map/all_to_all | solution.py:269
  76.5 2.4 %shard_map.128 = (bf16[512,1024]{1,0:T(8,128)(2,1)S(1)}, bf16[512,512]{1,0:T(8,128)(2,1)S(1)}, f32[256,128]{1,0:T(8,128)S(1)}) custom-call(s32[1,256]{1,0:T(1,128)S(1)} %bitcast.24, s32[15,1,256]{2,1,0:T(1,128)S(1)} %reshape.41.nbr_ref, s32[1,256]{1,0:T(1,128)S(1)} %bitcast.25, s32[256,128]{1,0:T(8,128)S(1)} %copy-done.9), custom_call_target="tpu_custom_call" | custom-call | flops 10485760 | bytes 2097152 | tf_op jit(solution)/shard_map/pallas_call | solution.py:30
  78.9 0.0 copy-start.4
  78.9 1.4 %copy-done.4 = bf16[768,1024]{1,0:T(8,128)(2,1)S(1)} copy-done((bf16[768,1024]{1,0:T(8,128)(2,1)S(1)}, bf16[768,1024]{1,0:T(8,128)(2,1)}, u32[]{:S(2)}) %copy-start.4) | copy-done | bytes 1572888
  80.3 1.4 %copy-done.5 = bf16[768,1024]{1,0:T(8,128)(2,1)S(1)} copy-done((bf16[768,1024]{1,0:T(8,128)(2,1)S(1)}, bf16[768,1024]{1,0:T(8,128)(2,1)}, u32[]{:S(2)}) %copy-start.5) | copy-done | bytes 1572888
  81.7 1.2 %shard_map.133 = (f32[512,768]{1,0:T(8,128)S(1)}, bf16[1536,1024]{1,0:T(8,128)(2,1)S(1)}, bf16[512,512]{1,0:T(8,128)(2,1)S(1)}) custom-call(bf16[768,1024]{1,0:T(8,128)(2,1)S(1)} %copy-done.4, bf16[768,1024]{1,0:T(8,128)(2,1)S(1)} %copy-done.5, bf16[512,1024]{1,0:T(8,128)(2,1)S(1)} %get-tuple-element.18.weight_ref, bf16[1024,768]{1,0:T(8,128)(2,1)S(1)} %bitcast.18, ...), custom_call_target="tpu_custom_call" | custom-call | flops 805306368 | bytes 8388608 | tf_op jit(solution)/shard_map/pallas_call | solution.py:30
  82.9 1.6 %copy-done.1 = bf16[1536,1024]{1,0:T(8,128)(2,1)} copy-done((bf16[1536,1024]{1,0:T(8,128)(2,1)}, bf16[1536,1024]{1,0:T(8,128)(2,1)S(1)}, u32[]{:S(2)}) %copy-start.1) | copy-done | bytes 3145752
  84.6 1.2 %copy-done.6 = f32[512,768]{1,0:T(8,128)} copy-done((f32[512,768]{1,0:T(8,128)}, f32[512,768]{1,0:T(8,128)S(1)}, u32[]{:S(2)}) %copy-start.6) | copy-done | bytes 1572888
  85.7 14.0 %all-to-all-done.2 = bf16[32,16,768]{2,1,0:T(8,128)(2,1)S(1)} async-done(((bf16[32,16,768]{2,1,0:T(8,128)(2,1)}), bf16[32,16,768]{2,1,0:T(8,128)(2,1)S(1)}, u32[]{:S(2)}, u32[]{:S(2)}) %all-to-all-start.2) | async-done | bytes 786464 | tf_op jit(solution)/shard_map/all_to_all | solution.py:269
  99.7 1.9 %copy-done.2 = bf16[1536,1024]{1,0:T(8,128)(2,1)S(1)} copy-done((bf16[1536,1024]{1,0:T(8,128)(2,1)S(1)}, bf16[1536,1024]{1,0:T(8,128)(2,1)}, u32[]{:S(2)}) %copy-start.2) | copy-done | bytes 3145752
  101.6 1.4 %copy-done.7 = f32[512,768]{1,0:T(8,128)S(1)} copy-done((f32[512,768]{1,0:T(8,128)S(1)}, f32[512,768]{1,0:T(8,128)}, u32[]{:S(2)}) %copy-start.7) | copy-done | bytes 1572888
  103.0 2.2 %shard_map.134 = bf16[256,1024]{1,0:T(8,128)(2,1)} custom-call(f32[512,768]{1,0:T(8,128)S(1)} %copy-done.7, bf16[512,512]{1,0:T(8,128)(2,1)S(1)} %get-tuple-element.25.weight_ref, bf16[512,768]{1,0:T(8,128)(2,1)S(1)} %bitcast.19, f32[256,128]{1,0:T(8,128)S(1)} %get-tuple-element.27.divisor_ref, bf16[1536,1024]{1,0:T(8,128)(2,1)S(1)} %copy-done.2, ...), custom_call_target="tpu_custom_call" | custom-call | flops 1207959552 | bytes 8388608 | tf_op jit(solution)/shard_map/pallas_call | solution.py:30
  (23 shorter events, 0.1 us)
Async XLA Ops:
  1.7 25.3 %all-to-all-start = ((s32[32,1,128]{2,1,0:T(1,128)}), s32[32,1,128]{2,1,0:T(1,128)S(1)}, u32[]{:S(2)}, u32[]{:S(2)}) async-start(s32[32,1,128]{2,1,0:T(1,128)} %get-tuple-element.19), calls=%async_computation | async-start | bytes 32768 | tf_op jit(solution)/shard_map/all_to_all | solution.py:235
  18.2 0.9 copy-start.8
  19.2 0.7 copy-start.11
  20.1 1.9 %copy-start = (bf16[2048,768]{1,0:T(8,128)(2,1)S(1)}, bf16[2048,768]{1,0:T(8,128)(2,1)}, u32[]{:S(2)}) copy-start(bf16[2048,768]{1,0:T(8,128)(2,1)} %vals_ref.3) | copy-start | bytes 9437188
  22.0 0.8 copy-start.10
  30.5 1.2 %copy-start.3 = (bf16[1024,768]{1,0:T(8,128)(2,1)}, bf16[1024,768]{1,0:T(8,128)(2,1)S(1)}, u32[]{:S(2)}) copy-start(bf16[1024,768]{1,0:T(8,128)(2,1)S(1)} %shard_map.132) | copy-start | bytes 4718596
  31.7 39.5 %all-to-all-start.1 = ((bf16[32,32,768]{2,1,0:T(8,128)(2,1)}), bf16[32,32,768]{2,1,0:T(8,128)(2,1)S(1)}, u32[]{:S(2)}, u32[]{:S(2)}) async-start(bf16[32,32,768]{2,1,0:T(8,128)(2,1)} %bitcast.20), calls=%async_computation.1 | async-start | bytes 3145728 | tf_op jit(solution)/shard_map/all_to_all | solution.py:247
  38.5 3.4 %collective-permute-start.2 = (bf16[128,768]{1,0:T(8,128)(2,1)S(1)}, bf16[128,768]{1,0:T(8,128)(2,1)S(1)}, u32[]{:S(2)}, u32[]{:S(2)}) collective-permute-start(bf16[128,768]{1,0:T(8,128)(2,1)S(1)} %shard_map.129), channel_id=1, source_target_pairs={{0,8},{33,41},{66,74},{99,107},{132,140},{165,173},{198,204},{231,... | collective-permute-start | bytes 589832 | tf_op jit(solution)/shard_map/ppermute | solution.py:196
  39.2 3.4 %collective-permute-start.1 = (bf16[128,768]{1,0:T(8,128)(2,1)S(1)}, bf16[128,768]{1,0:T(8,128)(2,1)S(1)}, u32[]{:S(2)}, u32[]{:S(2)}) collective-permute-start(bf16[128,768]{1,0:T(8,128)(2,1)S(1)} %shard_map.129), channel_id=1, source_target_pairs={{0,16},{33,49},{66,82},{99,115},{132,148},{165,181},{198,212},{231... | collective-permute-start | bytes 589832 | tf_op jit(solution)/shard_map/ppermute | solution.py:196
  39.9 2.8 %collective-permute-start = (bf16[128,768]{1,0:T(8,128)(2,1)S(1)}, bf16[128,768]{1,0:T(8,128)(2,1)S(1)}, u32[]{:S(2)}, u32[]{:S(2)}) collective-permute-start(bf16[128,768]{1,0:T(8,128)(2,1)S(1)} %shard_map.129), channel_id=1, source_target_pairs={{0,24},{33,57},{66,90},{99,123},{132,156},{165,189},{198,220},{231... | collective-permute-start | bytes 589832 | tf_op jit(solution)/shard_map/ppermute | solution.py:196
  40.6 3.5 %collective-permute-start.5 = (bf16[128,768]{1,0:T(8,128)(2,1)S(1)}, bf16[128,768]{1,0:T(8,128)(2,1)S(1)}, u32[]{:S(2)}, u32[]{:S(2)}) collective-permute-start(bf16[128,768]{1,0:T(8,128)(2,1)S(1)} %shard_map.129), channel_id=1, source_target_pairs={{0,2},{33,35},{66,64},{99,97},{132,128},{165,161},{198,192},{231,2... | collective-permute-start | bytes 589832 | tf_op jit(solution)/shard_map/ppermute | solution.py:196
  41.3 3.6 %collective-permute-start.4 = (bf16[128,768]{1,0:T(8,128)(2,1)S(1)}, bf16[128,768]{1,0:T(8,128)(2,1)S(1)}, u32[]{:S(2)}, u32[]{:S(2)}) collective-permute-start(bf16[128,768]{1,0:T(8,128)(2,1)S(1)} %shard_map.129), channel_id=1, source_target_pairs={{0,4},{33,37},{66,68},{99,101},{132,130},{165,163},{198,194},{231,... | collective-permute-start | bytes 589832 | tf_op jit(solution)/shard_map/ppermute | solution.py:196
  42.0 2.9 %collective-permute-start.3 = (bf16[128,768]{1,0:T(8,128)(2,1)S(1)}, bf16[128,768]{1,0:T(8,128)(2,1)S(1)}, u32[]{:S(2)}, u32[]{:S(2)}) collective-permute-start(bf16[128,768]{1,0:T(8,128)(2,1)S(1)} %shard_map.129), channel_id=1, source_target_pairs={{0,30},{33,63},{66,70},{99,103},{132,134},{165,167},{198,196},{231... | collective-permute-start | bytes 589832 | tf_op jit(solution)/shard_map/ppermute | solution.py:196
  42.7 2.1 %collective-permute-start.8 = (bf16[128,768]{1,0:T(8,128)(2,1)S(1)}, bf16[128,768]{1,0:T(8,128)(2,1)S(1)}, u32[]{:S(2)}, u32[]{:S(2)}) collective-permute-start(bf16[128,768]{1,0:T(8,128)(2,1)S(1)} %add_select_fusion.1), channel_id=1, source_target_pairs={{8,10},{16,18},{24,26},{41,43},{49,51},{57,59},{74,72},{82,80},{90... | collective-permute-start | bytes 589832 | tf_op jit(solution)/shard_map/ppermute | solution.py:196
  43.4 1.5 %collective-permute-start.7 = (bf16[128,768]{1,0:T(8,128)(2,1)S(1)}, bf16[128,768]{1,0:T(8,128)(2,1)S(1)}, u32[]{:S(2)}, u32[]{:S(2)}) collective-permute-start(bf16[128,768]{1,0:T(8,128)(2,1)S(1)} %add_select_fusion.1), channel_id=1, source_target_pairs={{8,12},{16,20},{24,28},{41,45},{49,53},{57,61},{74,76},{82,84},{90... | collective-permute-start | bytes 589832 | tf_op jit(solution)/shard_map/ppermute | solution.py:196
  44.1 0.8 collective-permute-start.6
  45.0 15.7 %collective-permute-start.9 = (bf16[128,768]{1,0:T(8,128)(2,1)S(1)}, bf16[128,768]{1,0:T(8,128)(2,1)S(1)}, u32[]{:S(2)}, u32[]{:S(2)}) collective-permute-start(bf16[128,768]{1,0:T(8,128)(2,1)S(1)} %add_select_fusion), channel_id=1, source_target_pairs={{0,1},{2,3},{4,5},{6,7},{8,9},{10,11},{12,13},{14,15},{16,17},{18,... | collective-permute-start | bytes 589832 | tf_op jit(solution)/shard_map/ppermute | solution.py:201
  46.3 30.1 %copy-start.15 = (s32[1,1,256,15]{2,1,3,0:T(1,128)S(1)}, s32[1,1,256,15]{2,1,3,0:T(1,128)}, u32[]{:S(2)}) copy-start(s32[1,1,256,15]{2,1,3,0:T(1,128)} %param.21) | copy-start | bytes 46084
  46.3 30.1 %copy-start.9 = (s32[256,128]{1,0:T(8,128)S(1)}, s32[256,128]{1,0:T(8,128)}, u32[]{:S(2)}) copy-start(s32[256,128]{1,0:T(8,128)} %get-tuple-element.17.place_ref) | copy-start | bytes 393220
  46.3 30.1 %copy-start.13 = (s32[1,1,256]{2,1,0:T(1,128)S(1)}, s32[1,1,256]{2,1,0:T(1,128)}, u32[]{:S(2)}) copy-start(s32[1,1,256]{2,1,0:T(1,128)} %param.20) | copy-start | bytes 3076
  46.3 30.1 %copy-start.14 = (s32[1,1,256]{2,1,0:T(1,128)S(1)}, s32[1,1,256]{2,1,0:T(1,128)}, u32[]{:S(2)}) copy-start(s32[1,1,256]{2,1,0:T(1,128)} %param.22) | copy-start | bytes 3076
  71.2 28.5 %all-to-all-start.2 = ((bf16[32,16,768]{2,1,0:T(8,128)(2,1)}), bf16[32,16,768]{2,1,0:T(8,128)(2,1)S(1)}, u32[]{:S(2)}, u32[]{:S(2)}) async-start(bf16[32,16,768]{2,1,0:T(8,128)(2,1)} %bitcast.10), calls=%async_computation.2 | async-start | bytes 1572864 | tf_op jit(solution)/shard_map/all_to_all | solution.py:269
  78.9 1.4 %copy-start.4 = (bf16[768,1024]{1,0:T(8,128)(2,1)S(1)}, bf16[768,1024]{1,0:T(8,128)(2,1)}, u32[]{:S(2)}) copy-start(bf16[768,1024]{1,0:T(8,128)(2,1)} %w_self_hbm.1) | copy-start | bytes 4718596
  80.3 1.4 %copy-start.5 = (bf16[768,1024]{1,0:T(8,128)(2,1)S(1)}, bf16[768,1024]{1,0:T(8,128)(2,1)}, u32[]{:S(2)}) copy-start(bf16[768,1024]{1,0:T(8,128)(2,1)} %w_nbr_hbm.1) | copy-start | bytes 4718596
  81.7 18.0 %copy-start.12 = (f32[1024]{0:T(1024)S(1)}, f32[1024]{0:T(1024)}, u32[]{:S(2)}) copy-start(f32[1024]{0:T(1024)} %param.25) | copy-start | bytes 12292
  82.9 1.6 %copy-start.1 = (bf16[1536,1024]{1,0:T(8,128)(2,1)}, bf16[1536,1024]{1,0:T(8,128)(2,1)S(1)}, u32[]{:S(2)}) copy-start(bf16[1536,1024]{1,0:T(8,128)(2,1)S(1)} %get-tuple-element.28.w_ref) | copy-start | bytes 9437188
  84.6 1.2 %copy-start.6 = (f32[512,768]{1,0:T(8,128)}, f32[512,768]{1,0:T(8,128)S(1)}, u32[]{:S(2)}) copy-start(f32[512,768]{1,0:T(8,128)S(1)} %get-tuple-element.24.part_ref) | copy-start | bytes 4718596
  99.7 1.9 %copy-start.2 = (bf16[1536,1024]{1,0:T(8,128)(2,1)S(1)}, bf16[1536,1024]{1,0:T(8,128)(2,1)}, u32[]{:S(2)}) copy-start(bf16[1536,1024]{1,0:T(8,128)(2,1)} %copy-done.1) | copy-start | bytes 9437188
  101.6 1.4 %copy-start.7 = (f32[512,768]{1,0:T(8,128)S(1)}, f32[512,768]{1,0:T(8,128)}, u32[]{:S(2)}) copy-start(f32[512,768]{1,0:T(8,128)} %copy-done.6) | copy-start | bytes 4718596
